TPU v7x, 32 devices: a whole 2x2x4 slice. The times are simulated.
32 devices in a mesh: circ: 4 (over z), mer: 8 (over y, x, core).
Axes of the slice: x: 2, y: 2, z: 4, core: 2. Of those that a mesh axis runs over, the one named last changes fastest.
Arguments:
- adjoint: float32 [6, 8, 2048], P(None, 'circ', 'mer'), may hold values from -6 to 6
- mode_fields: float32 [3, 6, 8, 2048], P(None, None, 'circ'), may hold values from -6 to 6
- node_slot: int32 [2048], replicated, may hold values from 0 to 2047, as said below
- thickness: float32 [8, 2048], P('circ'), may hold values from 0.5 to 1.5
- weld_land: int32 [8, 2048], P('circ'), may hold values 0 or 1
- panel_spans: int32 [4, 8], P('circ'), may hold values from 1 to 768, 2048 in all within a row
- load_factor: float32 [], replicated, may hold values from 0.5 to 1.5
- membrane: float32 [24, 24], replicated, may hold values from -1.25 to 1.25
- bending: float32 [24, 24], replicated, may hold values from -0.4375 to 0.4375
- geometric: float32 [3, 24, 24], replicated, may hold values from -1.25 to 1.25
- stress_map: float32 [3, 24], replicated, may hold values from -1.25 to 1.25
Outputs:
- adjoint_load: float32 [6, 8, 2048], P(None, 'circ', 'mer')
- thickness_grad: float32 [8, 6144], P('circ', 'mer')
Inputs may be any that keep to these rules, and one draw needn't show every extreme that they name: A permutation of the node positions; node_slot[j] // 256 equals j modulo 2048 // 256. `panel_spans`: each row sums to 2048 and its largest entry is 768.
All inputs are finite; a program needn't handle non-finite values. No bound on the sum of `weld_land` on one device may be relied on, other than what follows from the above.
Results may differ from a plain program's by a relative error of at most 0.0003.
Values sent between devices are 32-bit elements; how exact they have to be, the bound alone decides.
A program may use at most 128 MiB of HBM per device.

v0:
```python
import jax
import jax.numpy as jnp
from jax import lax
from jax.sharding import PartitionSpec as P

MOST = 768


highest = lax.Precision.HIGHEST


def from_behind(block, axis, distance):
    devices = range(lax.axis_size(axis))
    route = [((i - distance) % len(devices), i) for i in devices]
    return lax.ppermute(block, axis, route)


def element_terms(
    mode_vectors,
    adjoint_vectors,
    thick_rows,
    weld_rows,
    load_factor,
    membrane,
    bending,
    geometric,
    stress_map,
):
    land_growth = 1.0 + 0.5 * weld_rows
    thick_eff = thick_rows * land_growth
    membrane_part = jnp.einsum("ab,fbe->fae", membrane, mode_vectors, precision=highest)
    bending_part = jnp.einsum("ab,fbe->fae", bending, mode_vectors, precision=highest)
    tangent = membrane_part + 3.0 * thick_eff**2 * bending_part
    stiffness = jnp.sum(mode_vectors[0] * tangent[0] + mode_vectors[1] * tangent[1], axis=0)
    adjoint_term = jnp.sum(adjoint_vectors * tangent[2], axis=0)
    stress = jnp.dot(stress_map, mode_vectors[2], precision=highest)
    geometric_part = jnp.einsum("sab,kbe->ksae", geometric, mode_vectors[:2], precision=highest)
    pair_terms = jnp.sum(mode_vectors[:2, None] * geometric_part, axis=(0, 2))
    gradient = land_growth * (
        stiffness - load_factor * jnp.sum(stress * pair_terms, axis=0) - adjoint_term
    )
    load_rows = load_factor * thick_eff * jnp.dot(stress_map.T, pair_terms, precision=highest)
    return (gradient, load_rows)


def corner_values(field, upper_rim, cols_here, cols_next):
    lower_here = jnp.take(field, cols_here, axis=-1)
    lower_next = jnp.take(field, cols_next, axis=-1)
    rim_here = jnp.take(upper_rim, cols_here, axis=-1)
    rim_next = jnp.take(upper_rim, cols_next, axis=-1)
    upper_here = jnp.concatenate([lower_here[..., 1:, :], rim_here], axis=-2)
    upper_next = jnp.concatenate([lower_next[..., 1:, :], rim_next], axis=-2)
    return jnp.stack([lower_here, upper_here, upper_next, lower_next], axis=-4)


def on_device(
    adjoint,
    mode_fields,
    node_slot,
    thickness,
    weld_land,
    panel_spans,
    load_factor,
    membrane,
    bending,
    geometric,
    stress_map,
):
    cycle_count = adjoint.shape[1]
    owned_width = adjoint.shape[2]
    column_width = mode_fields.shape[3]
    block_width = min(128, owned_width)
    elements = cycle_count * block_width
    member = lax.axis_index("mer")
    group_size = lax.axis_size("mer")
    spans_row = panel_spans[0]
    span_count = spans_row[member]
    span_start = jnp.sum(jnp.where(jnp.arange(group_size, dtype=jnp.int32) < member, spans_row, 0))
    adj_column = lax.all_gather(adjoint, "mer", axis=2, tiled=True)
    adj_rim, mode_rim = from_behind((adj_column[:, :1], mode_fields[:, :, :1]), "circ", -1)
    cycle_ids = jnp.arange(cycle_count, dtype=jnp.int32)[:, None]

    def block_terms(accumulated, meridional, validity):
        cols_here = jnp.take(node_slot, meridional)
        cols_next = jnp.take(node_slot, (meridional + 1) % column_width)
        mode_vectors = corner_values(mode_fields, mode_rim, cols_here, cols_next).reshape(
            3, 24, elements
        )
        adjoint_vectors = corner_values(adj_column, adj_rim, cols_here, cols_next).reshape(
            24, elements
        )
        thick_rows = jnp.take(thickness, meridional, axis=1).reshape(elements)
        weld_rows = jnp.take(weld_land, meridional, axis=1).reshape(elements).astype(jnp.float32)
        gradient, load_rows = element_terms(
            mode_vectors,
            adjoint_vectors,
            thick_rows,
            weld_rows,
            load_factor,
            membrane,
            bending,
            geometric,
            stress_map,
        )
        load_rows = load_rows.reshape(4, 6, cycle_count, block_width) * validity
        accumulated = accumulated.at[:, cycle_ids, cols_here[None, :]].add(load_rows[0])
        accumulated = accumulated.at[:, cycle_ids + 1, cols_here[None, :]].add(load_rows[1])
        accumulated = accumulated.at[:, cycle_ids + 1, cols_next[None, :]].add(load_rows[2])
        accumulated = accumulated.at[:, cycle_ids, cols_next[None, :]].add(load_rows[3])
        return (accumulated, gradient.reshape(cycle_count, block_width) * validity)

    zero_loads = jnp.zeros((6, cycle_count + 1, column_width), jnp.float32)
    positions = jnp.arange(block_width, dtype=jnp.int32)

    def visit_even(block_index, carry):
        accumulated, gradients = carry
        offset = block_index * block_width + positions
        accumulated, gradient = block_terms(
            accumulated, member * owned_width + offset, jnp.ones((block_width,), jnp.float32)
        )
        gradients = lax.dynamic_update_slice_in_dim(
            gradients, gradient, block_index * block_width, 1
        )
        return (accumulated, gradients)

    accumulated, even_grad = lax.fori_loop(
        0,
        owned_width // block_width,
        visit_even,
        (zero_loads, jnp.zeros((cycle_count, owned_width), jnp.float32)),
    )
    column_grad = lax.all_gather(even_grad, "mer", axis=1, tiled=True)
    rolled = jnp.roll(column_grad, -span_start, axis=1)[:, :MOST]
    thickness_grad = rolled * (jnp.arange(MOST, dtype=jnp.int32) < span_count).astype(jnp.float32)
    reduced = lax.psum_scatter(accumulated, "mer", scatter_dimension=2, tiled=True)
    carried = from_behind(reduced[:, cycle_count:], "circ", 1)
    adjoint_load = reduced[:, :cycle_count].at[:, :1].add(carried)
    return (adjoint_load, thickness_grad)


def solution(mesh):
    return jax.shard_map(
        on_device,
        mesh=mesh,
        in_specs=(
            P(None, "circ", "mer"),
            P(None, None, "circ", None),
            P(),
            P("circ", None),
            P("circ", None),
            P("circ", None),
            P(),
            P(),
            P(),
            P(),
            P(),
        ),
        out_specs=(P(None, "circ", "mer"), P("circ", "mer")),
        check_vma=False,
    )
```

profile of v0, /device:TPU:0, one launch (start us, length us, event | category | flops | bytes accessed | tf_op | source)
XLA Modules:
  0.0 383.9 jit_solution(9373678938830549307)
XLA Ops:
  8.3 5.1 %collective-permute-start = (f32[3,6,1,2048]{3,2,1,0:T(1,128)S(1)}, f32[3,6,1,2048]{3,2,1,0:T(1,128)S(1)}, u32[]{:S(2)}, u32[]{:S(2)}) collective-permute-start(f32[3,6,1,2048]{3,2,1,0:T(1,128)S(1)} %slice.199), channel_id=1, source_target_pairs={{8,0},{16,8},{24,16},{0,24},{9,1},{17,9},{25,17},{1,25},{10,2},{18... | collective-permute-start | bytes 442376 | tf_op jit(solution)/shard_map/ppermute | solution.py:15
  13.4 9.1 %all_gather.6 = f32[6,2,2048]{2,1,0:T(2,128)S(1)} all-gather(f32[6,2,256]{2,1,0:T(2,128)} %param.25), channel_id=1, replica_groups=mesh['circ'=4,'mer'=8] {'mer'}, dimensions={2}, use_global_device_ids=true | all-gather | bytes 110592 | tf_op jit(solution)/shard_map/all_gather | solution.py:79
  24.2 8.2 %copy.267 = f32[3,6,2,2048]{1,2,3,0:T(2,128)} copy(f32[3,6,2,2048]{3,2,1,0:T(2,128)} %param.26) | data formatting | bytes 589824
  36.5 3.2 copy.268
  41.6 271.3 %while.20 = (s32[]{:T(128)}, f32[6,3,2048]{0,2,1:T(8,128)}, f32[2,256]{1,0:T(2,128)S(1)}, s32[]{:T(128)}, s32[2048]{0:T(1024)S(1)}, /*index=5*/f32[]{:T(128)}, f...) while((s32[]{:T(128)}, f32[6,3,2048]{0,2,1:T(8,128)}, ...), condition=%wide.region_9.15_spmd.clone.clone, body=%wide.region_0.14_spmd.clone.clone.sunk | while | flops 21971620 | bytes 2899831 | solution.py:126
  44.1 3.9 %gather_fusion.2 = f32[128,3,6,2]{2,3,1,0:T(2,128)S(1)} fusion(f32[3,6,2,2048]{1,2,3,0:T(2,128)} %get-tuple-element.949, s32[1024]{0:T(1024)S(1)} %pad_clamp_fusion.12), kind=kCustom, calls=%fused_computation.6.clone.clone.1 | custom fusion | bytes 37376 | tf_op jit(solution)/shard_map/while/body/eval_jaxpr/jit(_take)/gather | solution.py:48
  51.4 3.9 %gather_fusion.5 = f32[128,3,6,2]{2,3,1,0:T(2,128)S(1)} fusion(f32[3,6,2,2048]{1,2,3,0:T(2,128)} %get-tuple-element.949, s32[1024]{0:T(1024)S(1)} %pad_clamp_fusion.13), kind=kCustom, calls=%fused_computation.1.clone.clone.1 | custom fusion | bytes 37376 | tf_op jit(solution)/shard_map/while/body/eval_jaxpr/jit(_take)/gather | solution.py:47
  55.6 3.0 gather_fusion.4
  72.9 25.9 %scatter_fusion = f32[6,3,2048]{0,2,1:T(8,128)} fusion(f32[6,3,2048]{0,2,1:T(8,128)} %get-tuple-element.922, s32[256]{0:T(256)S(1)} %get-tuple-element.879, f32[256,6]{1,0:T(8,128)S(1)} %bitcast.238), kind=kCustom, calls=%fused_computation.12.clone.clone.1 | custom fusion | flops 1536 | bytes 20480 | tf_op jit(solution)/shard_map/while/body/eval_jaxpr/scatter-add | solution.py:106
  99.0 25.9 %scatter_fusion.1 = f32[6,3,2048]{0,2,1:T(8,128)} fusion(f32[6,3,2048]{0,2,1:T(8,128)} %scatter_fusion, s32[256]{0:T(256)S(1)} %get-tuple-element.885, f32[256,6]{1,0:T(8,128)S(1)} %bitcast.240), kind=kCustom, calls=%fused_computation.13.clone.clone.1 | custom fusion | flops 1536 | bytes 20480 | tf_op jit(solution)/shard_map/while/body/eval_jaxpr/scatter-add | solution.py:107
  125.1 26.0 %scatter_fusion.2 = f32[6,3,2048]{0,2,1:T(8,128)} fusion(f32[6,3,2048]{0,2,1:T(8,128)} %scatter_fusion.1, s32[256]{0:T(256)S(1)} %get-tuple-element.887, f32[256,6]{1,0:T(8,128)S(1)} %bitcast.241), kind=kCustom, calls=%fused_computation.14.clone.clone.1 | custom fusion | flops 1536 | bytes 20480 | tf_op jit(solution)/shard_map/while/body/eval_jaxpr/scatter-add | solution.py:108
  151.2 26.0 %scatter_fusion.3 = f32[6,3,2048]{0,2,1:T(8,128)} fusion(f32[6,3,2048]{0,2,1:T(8,128)} %scatter_fusion.2, s32[256]{0:T(256)S(1)} %get-tuple-element.889, f32[256,6]{1,0:T(8,128)S(1)} %bitcast.239), kind=kCustom, calls=%fused_computation.15.clone.clone.1 | custom fusion | flops 1536 | bytes 20480 | tf_op jit(solution)/shard_map/while/body/eval_jaxpr/scatter-add | solution.py:109
  179.6 3.9 %gather_fusion.2 = f32[128,3,6,2]{2,3,1,0:T(2,128)S(1)} fusion(f32[3,6,2,2048]{1,2,3,0:T(2,128)} %get-tuple-element.949, s32[1024]{0:T(1024)S(1)} %pad_clamp_fusion.12), kind=kCustom, calls=%fused_computation.6.clone.clone.1 | custom fusion | bytes 37376 | tf_op jit(solution)/shard_map/while/body/eval_jaxpr/jit(_take)/gather | solution.py:48
  183.8 3.0 gather_fusion.3
  186.9 3.9 %gather_fusion.5 = f32[128,3,6,2]{2,3,1,0:T(2,128)S(1)} fusion(f32[3,6,2,2048]{1,2,3,0:T(2,128)} %get-tuple-element.949, s32[1024]{0:T(1024)S(1)} %pad_clamp_fusion.13), kind=kCustom, calls=%fused_computation.1.clone.clone.1 | custom fusion | bytes 37376 | tf_op jit(solution)/shard_map/while/body/eval_jaxpr/jit(_take)/gather | solution.py:47
  191.1 3.0 gather_fusion.4
  208.4 26.0 %scatter_fusion = f32[6,3,2048]{0,2,1:T(8,128)} fusion(f32[6,3,2048]{0,2,1:T(8,128)} %get-tuple-element.922, s32[256]{0:T(256)S(1)} %get-tuple-element.879, f32[256,6]{1,0:T(8,128)S(1)} %bitcast.238), kind=kCustom, calls=%fused_computation.12.clone.clone.1 | custom fusion | flops 1536 | bytes 20480 | tf_op jit(solution)/shard_map/while/body/eval_jaxpr/scatter-add | solution.py:106
  234.5 26.0 %scatter_fusion.1 = f32[6,3,2048]{0,2,1:T(8,128)} fusion(f32[6,3,2048]{0,2,1:T(8,128)} %scatter_fusion, s32[256]{0:T(256)S(1)} %get-tuple-element.885, f32[256,6]{1,0:T(8,128)S(1)} %bitcast.240), kind=kCustom, calls=%fused_computation.13.clone.clone.1 | custom fusion | flops 1536 | bytes 20480 | tf_op jit(solution)/shard_map/while/body/eval_jaxpr/scatter-add | solution.py:107
  260.7 26.1 %scatter_fusion.2 = f32[6,3,2048]{0,2,1:T(8,128)} fusion(f32[6,3,2048]{0,2,1:T(8,128)} %scatter_fusion.1, s32[256]{0:T(256)S(1)} %get-tuple-element.887, f32[256,6]{1,0:T(8,128)S(1)} %bitcast.241), kind=kCustom, calls=%fused_computation.14.clone.clone.1 | custom fusion | flops 1536 | bytes 20480 | tf_op jit(solution)/shard_map/while/body/eval_jaxpr/scatter-add | solution.py:108
  286.9 26.0 %scatter_fusion.3 = f32[6,3,2048]{0,2,1:T(8,128)} fusion(f32[6,3,2048]{0,2,1:T(8,128)} %scatter_fusion.2, s32[256]{0:T(256)S(1)} %get-tuple-element.889, f32[256,6]{1,0:T(8,128)S(1)} %bitcast.239), kind=kCustom, calls=%fused_computation.15.clone.clone.1 | custom fusion | flops 1536 | bytes 20480 | tf_op jit(solution)/shard_map/while/body/eval_jaxpr/scatter-add | solution.py:109
  313.0 15.0 %copy.277 = f32[6,3,2048]{1,0,2:T(8,128)} copy(f32[6,3,2048]{0,2,1:T(8,128)} %get-tuple-element.451) | data formatting | bytes 294912
  328.0 6.2 %reshape.574 = f32[2048,18]{1,0:T(8,128)} reshape(f32[2048,6,3]{2,1,0:T(8,128)} %bitcast.231) | data formatting | bytes 294912
  337.4 9.3 %all_gather.7 = f32[2,2048]{1,0:T(2,128)S(1)} all-gather(f32[2,256]{1,0:T(2,128)S(1)} %get-tuple-element.452), channel_id=1, replica_groups=mesh['circ'=4,'mer'=8] {'mer'}, dimensions={1}, use_global_device_ids=true | all-gather | bytes 18432 | tf_op jit(solution)/shard_map/all_gather | solution.py:132
  346.7 22.4 %reduce-scatter.4.cloned.1.call-done = f32[256,18]{1,0:T(8,128)} async-done(((f32[2048,18]{1,0:T(8,128)}), f32[256,18]{1,0:T(8,128)}) %reduce-scatter.4.cloned.1.call-update) | async-done | bytes 18448
  (201 shorter events, 56.6 us)
Async XLA Ops:
  7.2 361.9 %reduce-scatter.4.cloned.1.call-start = ((), (), s32[]{:S(2)}) async-start(), calls=%async_computation.1 | async-start | bytes 1179648
  8.3 28.2 %collective-permute-start = (f32[3,6,1,2048]{3,2,1,0:T(1,128)S(1)}, f32[3,6,1,2048]{3,2,1,0:T(1,128)S(1)}, u32[]{:S(2)}, u32[]{:S(2)}) collective-permute-start(f32[3,6,1,2048]{3,2,1,0:T(1,128)S(1)} %slice.199), channel_id=1, source_target_pairs={{8,0},{16,8},{24,16},{0,24},{9,1},{17,9},{25,17},{1,25},{10,2},{18... | collective-permute-start | bytes 442376 | tf_op jit(solution)/shard_map/ppermute | solution.py:15
  22.6 12.5 %collective-permute-start.1 = (f32[6,1,2048]{2,1,0:T(1,128)S(1)}, f32[6,1,2048]{2,1,0:T(1,128)S(1)}, u32[]{:S(2)}, u32[]{:S(2)}) collective-permute-start(f32[6,1,2048]{2,1,0:T(1,128)S(1)} %slice.282), channel_id=1, source_target_pairs={{8,0},{16,8},{24,16},{0,24},{9,1},{17,9},{25,17},{1,25},{10,2},{18... | collective-permute-start | bytes 147464 | tf_op jit(solution)/shard_map/ppermute | solution.py:15
  24.2 8.2 %copy-start.5 = (f32[2,2048]{1,0:T(2,128)S(1)}, f32[2,2048]{1,0:T(2,128)}, u32[]{:S(2)}) copy-start(f32[2,2048]{1,0:T(2,128)} %param.28) | copy-start | bytes 49156
  24.2 9.6 %copy-start.6 = (s32[2,2048]{1,0:T(2,128)S(1)}, s32[2,2048]{1,0:T(2,128)}, u32[]{:S(2)}) copy-start(s32[2,2048]{1,0:T(2,128)} %param.29) | copy-start | bytes 49156
  36.5 5.2 %copy-start = (s32[2048]{0:T(1024)S(1)}, s32[2048]{0:T(1024)}, u32[]{:S(2)}) copy-start(s32[2048]{0:T(1024)} %param.27) | copy-start | bytes 24580
  36.5 5.2 %copy-start.1 = (f32[3,24,24]{2,1,0:T(8,128)S(1)}, f32[3,24,24]{2,1,0:T(8,128)}, u32[]{:S(2)}) copy-start(f32[3,24,24]{2,1,0:T(8,128)} %param.34) | copy-start | bytes 20740
  36.5 5.2 %copy-start.2 = (f32[24,24]{1,0:T(8,128)S(1)}, f32[24,24]{1,0:T(8,128)}, u32[]{:S(2)}) copy-start(f32[24,24]{1,0:T(8,128)} %param.33) | copy-start | bytes 6916
  36.5 5.2 %copy-start.3 = (f32[24,24]{1,0:T(8,128)S(1)}, f32[24,24]{1,0:T(8,128)}, u32[]{:S(2)}) copy-start(f32[24,24]{1,0:T(8,128)} %param.32) | copy-start | bytes 6916
  36.5 5.2 %copy-start.4 = (f32[3,24]{1,0:T(4,128)S(1)}, f32[3,24]{1,0:T(4,128)}, u32[]{:S(2)}) copy-start(f32[3,24]{1,0:T(4,128)} %param.35) | copy-start | bytes 868
  328.0 6.2 %copy-start.8 = (s32[1,8]{1,0:T(1,128)S(1)}, s32[1,8]{1,0:T(1,128)}, u32[]{:S(2)}) copy-start(s32[1,8]{1,0:T(1,128)} %param.30) | copy-start | bytes 100
  370.9 5.5 %collective-permute-start.2 = (f32[6,1,256]{2,1,0:T(1,128)S(1)}, f32[6,1,256]{2,1,0:T(1,128)S(1)}, u32[]{:S(2)}, u32[]{:S(2)}) collective-permute-start(f32[6,1,256]{2,1,0:T(1,128)S(1)} %copy.282), channel_id=1, source_target_pairs={{24,0},{0,8},{8,16},{16,24},{25,1},{1,9},{9,17},{17,25},{26,2},{2,... | collective-permute-start | bytes 18440 | tf_op jit(solution)/shard_map/ppermute | solution.py:15
  376.4 0.6 copy-start.7
Sparse Core Ops, SparseCore 0:
  334.3 34.7 reduce-scatter.3
where the time goes:
time: 390 us; the launch traced here: 384 us
  other arithmetic  216 us (55%)
  local copies, waits for them, and re-layouts  98.5 us (25%)
  waiting for transfers between devices  25 us (6%)
  blocking collectives  18.4 us (5%)
  between operations  15.5 us (4%)
  starting transfers between devices  7.16 us (2%)
    scatter-add x2, other arithmetic, block_terms(): accumulated.at[:, cycle_ids + 1, cols_next[None, :]].add(load_rows[2])  52 us
    scatter-add x2, other arithmetic, block_terms(): accumulated.at[:, cycle_ids, cols_next[None, :]].add(load_rows[3])  52 us
    scatter-add x2, other arithmetic, block_terms(): accumulated.at[:, cycle_ids + 1, cols_here[None, :]].add(load_rows[1])  51.9 us
    scatter-add x2, other arithmetic, block_terms(): accumulated.at[:, cycle_ids, cols_here[None, :]].add(load_rows[0])  51.9 us
    unnamed x30, local copies, waits for them, and re-layouts  40.5 us
    unnamed x2, waiting for transfers between devices  22.4 us
    gather x6, local copies, waits for them, and re-layouts, corner_values(): rim_here = jnp.take(upper_rim, cols_here, axis=-1)  9.83 us
    gather x6, local copies, waits for them, and re-layouts, corner_values(): rim_next = jnp.take(upper_rim, cols_next, axis=-1)  9.83 us
  transfers between devices with their start and end apart: 4, of which 2 were waited for; matrix products, arithmetic and copies ran while one was open for 4% of the time, Pallas kernels for 0%

commit v1 on v0

v1 whole, which is shorter than its diff:
```python
import functools
import jax
import jax.numpy as jnp
from jax import lax
from jax.experimental import pallas as pl
from jax.experimental.pallas import tpu as pltpu
from jax.sharding import PartitionSpec as P

MOST = 768
LANES = 128
WIDE = 256


def lane_gather(x, index):
    return jnp.take_along_axis(x, index, axis=1, mode="promise_in_bounds")


def split(x):
    high = x.astype(jnp.bfloat16).astype(jnp.float32)
    return high, x - high


def gather_wide(block, low_index, in_low):
    left = lane_gather(block[:, :LANES], low_index)
    right = lane_gather(block[:, LANES:], low_index)
    return jnp.where(in_low, left, right)


def iota(shape, axis):
    return lax.broadcasted_iota(jnp.int32, shape, axis)


def untangle(turned, column, positions, groups, stride=1):
    width = LANES // groups
    tile = (positions // width) * stride + column
    within = positions % width
    parts = []
    for eight in range(groups // 8):
        total = None
        for q in range(width):
            base = groups * q + 8 * eight
            picked = lane_gather(turned[base : base + 8, :], tile)
            total = picked if total is None else jnp.where(within == q, picked, total)
        parts.append(total)
    return parts


def down(x):
    return jnp.sum(x, axis=0, keepdims=True)


def stack_corners(lower_here, upper_here, upper_next, lower_next):
    return jnp.concatenate([lower_here, upper_here, upper_next, lower_next], axis=0)


def triple(v):
    high, low = split(v)
    return jnp.concatenate([high, high, low], axis=0)


def mm(a, b):
    return jnp.dot(a, b, preferred_element_type=jnp.float32)


def local_kernel(
    groups, tiles, slot_ref, span_ref, factor_ref, thick_ref, weld_ref, nodes_ref, mats_ref, map_ref,
    load_ref, carry_ref, grad_ref,
    index_ref, teff_ref, window_ref, near_ref, xy_ref,
):
    member = lax.axis_index("mer")
    factor = factor_ref[0]
    start = jnp.int32(0)
    count = jnp.int32(0)
    for g in range(groups):
        start = start + jnp.where(g < member, span_ref[0, g], 0)
        count = count + jnp.where(g == member, span_ref[0, g], 0)
    first = start // groups
    lane = iota((8, LANES), 1)

    pad = jnp.zeros((LANES - tiles, LANES), jnp.int32)
    slots = jnp.concatenate([slot_ref[...], pad], axis=0) % WIDE
    slots_t = slots.astype(jnp.float32).T.astype(jnp.int32)
    for half in range(2):
        for e, part in enumerate(untangle(slots_t, 0, lane + half * LANES, groups)):
            index_ref[8 * e : 8 * e + 8, half * LANES : (half + 1) * LANES] = part
    shifted = untangle(slots_t, 0, (first + lane) % WIDE, groups)

    growth = 1.0 + 0.5 * weld_ref[...].astype(jnp.float32)
    effective = thick_ref[...] * growth
    for cycle in range(2):
        rows = [effective[cycle : cycle + 1, t * LANES : (t + 1) * LANES] for t in range(tiles)]
        natural = jnp.concatenate(rows + [jnp.zeros((LANES - tiles, LANES), jnp.float32)], axis=0)
        natural_t = natural.T
        for half in range(2):
            for e, part in enumerate(untangle(natural_t, 0, lane + half * LANES, groups)):
                teff_ref[cycle, 8 * e : 8 * e + 8, half * LANES : (half + 1) * LANES] = part

    a_high, a_low = split(mats_ref[...])
    mats = jnp.concatenate([a_high, a_low, a_high], axis=1)

    owners, rows_of = [], []
    for d in (-1, 0, 1):
        owner = lax.rem(member + d + groups, groups)
        row = index_ref[pl.ds(owner, 1), :]
        if d == -1:
            row = jnp.where(member == 0, pltpu.roll(row, 1, 1), row)
        if d == 1:
            row = jnp.where(member == groups - 1, pltpu.roll(row, WIDE - 1, 1), row)
        owners.append(owner)
        rows_of.append(row)
    for d in range(3):
        base = pl.multiple_of(owners[d] * WIDE, WIDE)
        wide = jnp.broadcast_to(rows_of[d], (8, WIDE))
        for half in range(2):
            index = wide[:, half * LANES : (half + 1) * LANES]
            low, in_low = index % LANES, index < LANES
            for q in range(3):
                for f in range(2):
                    block = nodes_ref[q, 8 * f : 8 * f + 8, pl.ds(base, WIDE)]
                    near_ref[q, 8 * f : 8 * f + 8, d * WIDE + half * LANES : d * WIDE + (half + 1) * LANES] = (
                        gather_wide(block, low, in_low)
                    )
    loads = [jnp.zeros((8, WIDE), jnp.float32) for _ in range(3)]
    for r in range(2):
        pair = [0.0, 0.0, 0.0]
        for f in range(2):
            rows = slice(8 * f, 8 * f + 8)
            v = stack_corners(
                near_ref[r, rows, : 2 * WIDE],
                near_ref[r + 1, rows, : 2 * WIDE],
                near_ref[r + 1, rows, WIDE:],
                near_ref[r, rows, WIDE:],
            )
            product = mm(mats[64:160], triple(v))
            for s in range(3):
                pair[s] = pair[s] + down(v * product[32 * s : 32 * s + 32])
        spread = 0.0
        for s in range(3):
            spread = spread + map_ref[:, s : s + 1] * pair[s]
        behind = lax.rem(member + groups - 1, groups)
        te_here = teff_ref[r, pl.ds(member, 1), :]
        te_behind = teff_ref[r, pl.ds(behind, 1), :]
        te_behind = jnp.where(member == 0, pltpu.roll(te_behind, 1, 1), te_behind)
        from_behind_ = spread[:, :WIDE] * (factor * te_behind)
        from_here = spread[:, WIDE:] * (factor * te_here)
        loads[r] = loads[r] + from_here[0:8] + from_behind_[24:32]
        loads[r + 1] = loads[r + 1] + from_here[8:16] + from_behind_[16:24]
    values = jnp.concatenate(loads, axis=0)
    high, rest = split(values)
    middle, low3 = split(rest)
    place = (iota((WIDE, WIDE), 0) == jnp.broadcast_to(rows_of[1], (WIDE, WIDE))).astype(jnp.float32)
    placed = lax.dot_general(
        jnp.concatenate([high, middle, low3], axis=0), place, (((1,), (1,)), ((), ())),
        preferred_element_type=jnp.float32,
    )
    placed = placed[0:24] + placed[24:48] + placed[48:72]
    load_ref[0] = placed[0:8]
    load_ref[1] = placed[8:16]
    carry_ref[...] = placed[16:24]

    for o in range(groups):
        index = jnp.broadcast_to(shifted[o // 8][o % 8 : o % 8 + 1, :], (8, LANES))
        low, in_low = index % LANES, index < LANES
        for q in range(3):
            for f in range(4):
                block = nodes_ref[q, 8 * f : 8 * f + 8, o * WIDE : (o + 1) * WIDE]
                got = gather_wide(block, low, in_low)
                window_ref[q, 8 * f : 8 * f + 8, o * LANES : (o + 1) * LANES] = got
                if o == 0:
                    window_ref[q, 8 * f : 8 * f + 8, groups * LANES : (groups + 1) * LANES] = pltpu.roll(
                        got, LANES - 1, 1
                    )
    size = 8 * LANES
    for r in range(2):
        for part in range(groups // 8):
            here = slice(part * size, (part + 1) * size)
            after = slice(part * size + LANES, (part + 1) * size + LANES)

            def corner(f):
                rows = slice(8 * f, 8 * f + 8)
                return stack_corners(
                    window_ref[r, rows, here],
                    window_ref[r + 1, rows, here],
                    window_ref[r + 1, rows, after],
                    window_ref[r, rows, after],
                )

            quad = [0.0] * 5
            for f in range(2):
                v = corner(f)
                product = mm(mats, triple(v))[:160]
                for s in range(5):
                    quad[s] = quad[s] + v * product[32 * s : 32 * s + 32]
            u, a = corner(2), corner(3)
            u_three = triple(u)
            tangent = mm(mats[0:64], u_three)
            stress = mm(mats[160:168], u_three)
            geometric = 0.0
            for s in range(3):
                geometric = geometric + stress[s : s + 1] * down(quad[2 + s])
            x = down(quad[0] - a * tangent[0:32]) - factor * geometric
            y = down(quad[1] - a * tangent[32:64])
            for o in range(8):
                cut = slice(o * LANES, (o + 1) * LANES)
                xy_ref[2 * r, 8 * part + o : 8 * part + o + 1, :] = x[:, cut]
                xy_ref[2 * r + 1, 8 * part + o : 8 * part + o + 1, :] = y[:, cut]

    width = thick_ref.shape[1]
    back = lax.rem(width - start, width)
    te_span = pltpu.roll(effective, back, 1)[:, :MOST]
    growth_span = pltpu.roll(growth, back, 1)[:, :MOST]
    offset = start - first * groups
    sub = iota((8, LANES), 0)
    for b in range(MOST // LANES):
        n = lane + (b * LANES + offset)
        o_of, k_of = n % groups, n // groups
        cut = slice(b * LANES, (b + 1) * LANES)
        keep = lane[0:1] + b * LANES < count
        for r in range(2):
            both = []
            for z in range(2):
                total = 0.0
                for e in range(groups // 8):
                    picked = lane_gather(xy_ref[2 * r + z, 8 * e : 8 * e + 8, :], k_of)
                    total = total + jnp.sum(jnp.where(o_of == sub + 8 * e, picked, 0.0), axis=0, keepdims=True)
                both.append(total)
            te = te_span[r : r + 1, cut]
            g = growth_span[r : r + 1, cut] * (both[0] + 3.0 * te * te * both[1])
            grad_ref[r : r + 1, cut] = jnp.where(keep, g, 0.0)


def padded_mats(membrane, bending, geometric, stress_map):
    square = jnp.concatenate([membrane[None], bending[None], geometric], axis=0).reshape(5, 4, 6, 4, 6)
    square = jnp.pad(square, ((0, 0), (0, 0), (0, 2), (0, 0), (0, 2))).reshape(160, 32)
    rows = jnp.pad(stress_map.reshape(3, 4, 6), ((0, 5), (0, 0), (0, 2))).reshape(8, 32)
    return jnp.concatenate([square, rows], axis=0), rows.T


def on_device(
    adjoint, mode_fields, node_slot, thickness, weld_land, panel_spans, load_factor,
    membrane, bending, geometric, stress_map,
):
    column_width = mode_fields.shape[3]
    groups = lax.axis_size("mer")
    rings = lax.axis_size("circ")
    tiles = column_width // LANES
    adj_column = lax.all_gather(adjoint, "mer", axis=2, tiled=True)
    whole = jnp.concatenate([mode_fields, adj_column[None]], axis=0)
    whole = jnp.pad(jnp.transpose(whole, (2, 0, 1, 3)), ((0, 0), (0, 0), (0, 2), (0, 0))).reshape(2, 32, column_width)
    rim = lax.ppermute(whole[:1], "circ", [((i + 1) % rings, i) for i in range(rings)])
    nodes = jnp.concatenate([whole, rim], axis=0)
    mats, map_t = padded_mats(membrane, bending, geometric, stress_map)
    vmem = pl.BlockSpec(memory_space=pltpu.VMEM)
    smem = pl.BlockSpec(memory_space=pltpu.SMEM)
    load, carry, grad = pl.pallas_call(
        functools.partial(local_kernel, groups, tiles),
        out_shape=(
            jax.ShapeDtypeStruct((2, 8, WIDE), jnp.float32),
            jax.ShapeDtypeStruct((8, WIDE), jnp.float32),
            jax.ShapeDtypeStruct((2, MOST), jnp.float32),
        ),
        in_specs=[vmem, smem, smem, vmem, vmem, vmem, vmem, vmem],
        out_specs=(vmem, vmem, vmem),
        scratch_shapes=[
            pltpu.VMEM((groups, WIDE), jnp.int32),
            pltpu.VMEM((2, groups, WIDE), jnp.float32),
            pltpu.VMEM((3, 32, (groups + 1) * LANES), jnp.float32),
            pltpu.VMEM((3, 16, 3 * WIDE), jnp.float32),
            pltpu.VMEM((4, groups, LANES), jnp.float32),
        ],
        compiler_params=pltpu.CompilerParams(vmem_limit_bytes=32 * 1024 * 1024),
    )(
        node_slot.reshape(tiles, LANES), panel_spans, load_factor.reshape(1), thickness, weld_land,
        nodes, mats, map_t,
    )
    carried = lax.ppermute(carry, "circ", [(i, (i + 1) % rings) for i in range(rings)])
    load = load.at[0].add(carried)
    adjoint_load = jnp.transpose(load[:, :6], (1, 0, 2))
    return (adjoint_load, grad)


def solution(mesh):
    return jax.shard_map(
        on_device,
        mesh=mesh,
        in_specs=(
            P(None, "circ", "mer"),
            P(None, None, "circ", None),
            P(),
            P("circ", None),
            P("circ", None),
            P("circ", None),
            P(),
            P(),
            P(),
            P(),
            P(),
        ),
        out_specs=(P(None, "circ", "mer"), P("circ", "mer")),
        check_vma=False,
    )
```

time: 390 us -> 33.3 us (0.09); the launches traced: 384 us -> 32.8 us
  other arithmetic: 216 us -> 1.43 us
  local copies, waits for them, and re-layouts: 98.5 us -> 4.63 us
  waiting for transfers between devices: 25 us -> 7.52 us
  between operations: 15.5 us -> 1.41 us
  blocking collectives: 18.4 us -> 10.6 us
    scatter-add x8 -> x1, other arithmetic: 208 us -> 0.01 us  [on_device(): load = load.at[0].add(carried)]
    gather x36 -> x0, local copies, waits for them, and re-layouts: 51.6 us -> none  [the longest x6 9.83 us: corner_values(): rim_here = jnp.take(upper_rim, cols_here, axis=-1)]
    unnamed x30 -> x20, local copies, waits for them, and re-layouts: 40.5 us -> 2.93 us
    unnamed x2 -> x0, waiting for transfers between devices: 22.4 us -> none
    all_gather x1 -> x0, blocking collectives: 9.3 us -> none  [on_device(): column_grad = lax.all_gather(even_grad, 'mer', axis=1, tiled=True)]
    ppermute x3 -> x2, waiting for transfers between devices: 2.61 us -> 7.52 us  [the longest x1 5.45 us: on_device(): lax.ppermute(carry, 'circ', [(i, (i + 1) % rings) for i in range(rings)])]
  transfers between devices with their start and end apart: 4 -> 2, of which waited for: 2 -> 2; matrix products, arithmetic and copies ran while one was open for 4% -> 6% of each run, Pallas kernels for 0% -> 0%
where the time goes in v1:
time: 33.3 us; the launch traced here: 32.8 us
  blocking collectives  10.6 us (32%)
  waiting for transfers between devices  7.52 us (23%)
  local copies, waits for them, and re-layouts  4.63 us (14%)
  starting transfers between devices  4.11 us (12%)
  Pallas kernels  3.06 us (9%)
  other arithmetic  1.43 us (4%)
  between operations  1.41 us (4%)
    all_gather x1, blocking collectives, on_device(): adj_column = lax.all_gather(adjoint, 'mer', axis=2, tiled=True)  10.6 us
    ppermute x1, waiting for transfers between devices, on_device(): lax.ppermute(carry, 'circ', [(i, (i + 1) % rings) for i in range(rings)])  5.45 us
    ppermute x1, starting transfers between devices, on_device(): lax.ppermute(whole[:1], 'circ', [((i + 1) % rings, i) for i in range(ring...  3.65 us
    pallas_call x1, Pallas kernels, on_device(): pl.pallas_call(functools.partial(local_kernel, groups, tiles), out_shape=...  3.06 us
    unnamed x20, local copies, waits for them, and re-layouts  2.93 us
    ppermute x1, waiting for transfers between devices, on_device(): lax.ppermute(whole[:1], 'circ', [((i + 1) % rings, i) for i in range(ring...  2.07 us
    transpose x1, other arithmetic, on_device(): jnp.transpose(whole, (2, 0, 1, 3))  1.18 us
    concatenate x6, local copies, waits for them, and re-layouts, padded_mats(): jnp.concatenate([membrane[None], bending[None], geometric], axis=0)  1.12 us
  transfers between devices with their start and end apart: 2, of which 2 were waited for; matrix products, arithmetic and copies ran while one was open for 6% of the time, Pallas kernels for 0%

profile of v1, /device:TPU:0, one launch (start us, length us, event | category | flops | bytes accessed | tf_op | source)
XLA Modules:
  0.0 32.8 jit_solution(6347682868317977230)
XLA Ops:
  0.6 10.6 %all_gather.3 = f32[6,2,2048]{2,1,0:T(2,128)S(1)} all-gather(f32[6,2,256]{2,1,0:T(2,128)} %param.13), channel_id=1, replica_groups=mesh['circ'=4,'mer'=8] {'mer'}, dimensions={2}, use_global_device_ids=true | all-gather | bytes 110592 | tf_op jit(solution)/shard_map/all_gather | solution.py:247
  11.2 1.2 %maximum_bitcast_fusion = f32[2,4,6,2048]{3,0,2,1:T(2,128)S(1)} fusion(f32[1,6,2,2048]{3,2,1,0:T(2,128)S(1)} %bitcast.27, f32[3,6,2,2048]{3,2,1,0:T(2,128)} %param.14), kind=kLoop, calls=%fused_computation.2 | loop fusion | flops 98304 | bytes 786432 | tf_op jit(solution)/shard_map/transpose | solution.py:249
  12.4 0.2 pad_slice_fusion
  12.6 0.1 copy.37
  12.7 3.7 %collective-permute-start = (f32[1,32,2048]{2,1,0:T(8,128)S(1)}, f32[1,32,2048]{2,1,0:T(8,128)S(1)}, u32[]{:S(2)}, u32[]{:S(2)}) collective-permute-start(f32[1,32,2048]{2,1,0:T(8,128)S(1)} %bitcast.28), channel_id=1, source_target_pairs={{8,0},{16,8},{24,16},{0,24},{9,1},{17,9},{25,17},{1,25},{10,2},{18... | collective-permute-start | bytes 786440 | tf_op jit(solution)/shard_map/ppermute | solution.py:250
  16.4 0.1 concatenate.25
  16.5 0.4 %copy.28 = f32[3,4,6,4,6]{2,1,0,4,3:T(4,128)S(1)} copy(f32[3,4,6,4,6]{4,3,2,1,0:T(4,128)S(1)} %concatenate.25) | data formatting | bytes 13824 | tf_op jit(solution)/shard_map/concatenate | solution.py:233
  16.9 0.3 copy-done.5
  17.2 0.1 concatenate.23
  17.3 0.2 copy.26
  17.5 0.5 %copy-done.6 = f32[24,24]{1,0:T(8,128)S(1)} copy-done((f32[24,24]{1,0:T(8,128)S(1)}, f32[24,24]{1,0:T(8,128)}, u32[]{:S(2)}) %copy-start.6) | copy-done | bytes 2328
  18.1 0.2 copy.27
  18.3 0.1 select_maximum_fusion
  18.4 0.2 copy.38
  18.7 0.4 %copy-done.7 = f32[3,24]{1,0:T(4,128)S(1)} copy-done((f32[3,24]{1,0:T(4,128)S(1)}, f32[3,24]{1,0:T(4,128)}, u32[]{:S(2)}) %copy-start.7) | copy-done | bytes 312
  19.2 0.1 copy.33
  19.3 0.2 reshape.65
  19.6 0.1 copy.30.mats_ref
  20.4 2.1 %collective-permute-done = f32[1,32,2048]{2,1,0:T(8,128)S(1)} collective-permute-done((f32[1,32,2048]{2,1,0:T(8,128)S(1)}, f32[1,32,2048]{2,1,0:T(8,128)S(1)}, u32[]{:S(2)}, u32[]{:S(2)}) %collective-permute-start) | collective-permute-done | bytes 262176 | tf_op jit(solution)/shard_map/ppermute | solution.py:250
  22.5 0.6 %copy-done = f32[2,2048]{1,0:T(2,128)S(1)} copy-done((f32[2,2048]{1,0:T(2,128)S(1)}, f32[2,2048]{1,0:T(2,128)}, u32[]{:S(2)}) %copy-start) | copy-done | bytes 16408
  23.2 3.1 %shard_map.122 = (f32[2,8,256]{2,1,0:T(8,128)S(1)}, f32[8,256]{1,0:T(8,128)S(1)}, f32[2,768]{1,0:T(2,128)}) custom-call(s32[16,128]{1,0:T(8,128)S(1)} %bitcast.25, s32[1,8]{1,0:T(1,128)S(1)} %copy-done.3, f32[1]{0:T(128)} %bitcast.24.factor_ref, f32[2,2048]{1,0:T(2,128)S(1)} %copy-done, s32[2,2048]{1,0:T(2,128)S(1)} %copy-done.1, ...), custom_call_target="tpu_custom_call" | custom-call | tf_op jit(solution)/shard_map/pallas_call | solution.py:255
  26.2 0.5 %collective-permute-start.1 = (f32[8,256]{1,0:T(8,128)S(1)}, f32[8,256]{1,0:T(8,128)S(1)}, u32[]{:S(2)}, u32[]{:S(2)}) collective-permute-start(f32[8,256]{1,0:T(8,128)S(1)} %get-tuple-element.18), channel_id=1, source_target_pairs={{0,8},{8,16},{16,24},{24,0},{1,9},{9,17},{17,25},{25,1},{2,10},{10... | collective-permute-start | bytes 24584 | tf_op jit(solution)/shard_map/ppermute | solution.py:276
  26.7 5.5 %collective-permute-done.1 = f32[8,256]{1,0:T(8,128)S(1)} collective-permute-done((f32[8,256]{1,0:T(8,128)S(1)}, f32[8,256]{1,0:T(8,128)S(1)}, u32[]{:S(2)}, u32[]{:S(2)}) %collective-permute-start.1) | collective-permute-done | bytes 8224 | tf_op jit(solution)/shard_map/ppermute | solution.py:276
  32.2 0.6 %copy.31 = f32[6,2,256]{2,1,0:T(2,128)} copy(f32[6,2,256]{2,0,1:T(8,128)S(1)} %slice_bitcast_fusion) | data formatting | bytes 24576
  (20 shorter events, 0.4 us)
Async XLA Ops:
  12.6 3.8 %copy-start.4 = (f32[3,24,24]{2,1,0:T(8,128)S(1)}, f32[3,24,24]{2,1,0:T(8,128)}, u32[]{:S(2)}) copy-start(f32[3,24,24]{2,1,0:T(8,128)} %param.22) | copy-start | bytes 20740
  12.7 9.7 %collective-permute-start = (f32[1,32,2048]{2,1,0:T(8,128)S(1)}, f32[1,32,2048]{2,1,0:T(8,128)S(1)}, u32[]{:S(2)}, u32[]{:S(2)}) collective-permute-start(f32[1,32,2048]{2,1,0:T(8,128)S(1)} %bitcast.28), channel_id=1, source_target_pairs={{8,0},{16,8},{24,16},{0,24},{9,1},{17,9},{25,17},{1,25},{10,2},{18... | collective-permute-start | bytes 786440 | tf_op jit(solution)/shard_map/ppermute | solution.py:250
  16.5 0.7 %copy-start.5 = (f32[24,24]{1,0:T(8,128)S(1)}, f32[24,24]{1,0:T(8,128)}, u32[]{:S(2)}) copy-start(f32[24,24]{1,0:T(8,128)} %param.20) | copy-start | bytes 6916
  17.3 0.7 %copy-start.6 = (f32[24,24]{1,0:T(8,128)S(1)}, f32[24,24]{1,0:T(8,128)}, u32[]{:S(2)}) copy-start(f32[24,24]{1,0:T(8,128)} %param.21) | copy-start | bytes 6916
  18.4 0.7 %copy-start.7 = (f32[3,24]{1,0:T(4,128)S(1)}, f32[3,24]{1,0:T(4,128)}, u32[]{:S(2)}) copy-start(f32[3,24]{1,0:T(4,128)} %param.23) | copy-start | bytes 868
  22.4 0.7 %copy-start = (f32[2,2048]{1,0:T(2,128)S(1)}, f32[2,2048]{1,0:T(2,128)}, u32[]{:S(2)}) copy-start(f32[2,2048]{1,0:T(2,128)} %thick_ref.1) | copy-start | bytes 49156
  22.4 0.7 %copy-start.1 = (s32[2,2048]{1,0:T(2,128)S(1)}, s32[2,2048]{1,0:T(2,128)}, u32[]{:S(2)}) copy-start(s32[2,2048]{1,0:T(2,128)} %weld_ref.1) | copy-start | bytes 49156
  22.4 0.7 %copy-start.2 = (s32[2048]{0:T(1024)S(1)}, s32[2048]{0:T(1024)}, u32[]{:S(2)}) copy-start(s32[2048]{0:T(1024)} %param.15) | copy-start | bytes 24580
  22.5 0.7 %copy-start.3 = (s32[1,8]{1,0:T(1,128)S(1)}, s32[1,8]{1,0:T(1,128)}, u32[]{:S(2)}) copy-start(s32[1,8]{1,0:T(1,128)} %span_ref.1) | copy-start | bytes 100
  26.2 5.9 %collective-permute-start.1 = (f32[8,256]{1,0:T(8,128)S(1)}, f32[8,256]{1,0:T(8,128)S(1)}, u32[]{:S(2)}, u32[]{:S(2)}) collective-permute-start(f32[8,256]{1,0:T(8,128)S(1)} %get-tuple-element.18), channel_id=1, source_target_pairs={{0,8},{8,16},{16,24},{24,0},{1,9},{9,17},{17,25},{25,1},{2,10},{10... | collective-permute-start | bytes 24584 | tf_op jit(solution)/shard_map/ppermute | solution.py:276

commit v2 on v1

--- a/solution.py
+++ b/solution.py
@@ -58,17 +58,122 @@
     return jnp.concatenate([high, high, low], axis=0)
 
 
+def nt(a, b):
+    return lax.dot_general(a, b, (((1,), (1,)), ((), ())), preferred_element_type=jnp.float32)
+
+
 def mm(a, b):
     return jnp.dot(a, b, preferred_element_type=jnp.float32)
 
 
-def local_kernel(
-    groups, tiles, slot_ref, span_ref, factor_ref, thick_ref, weld_ref, nodes_ref, mats_ref, map_ref,
-    load_ref, carry_ref, grad_ref,
-    index_ref, teff_ref, window_ref, near_ref, xy_ref,
+def prepared_mats(membrane, bending, geometric, stress_map):
+    stress = jnp.concatenate([stress_map, jnp.zeros((5, 24), jnp.float32)], axis=0)
+    stacked = jnp.concatenate([membrane, bending, geometric[0], geometric[1], geometric[2], stress], axis=0)
+    high, low = split(stacked)
+    i, j = iota((24, 96), 0), iota((24, 96), 1)
+    lands = (j % 8 < 6) & (i == 6 * (j % 32 // 8) + j % 8)
+    from_low = j // 32 == 1
+    put_high = jnp.where(lands & jnp.logical_not(from_low), 1.0, 0.0)
+    put_low = jnp.where(lands & from_low, 1.0, 0.0)
+    wide = mm(high, put_high) + mm(low, put_low)
+    row, source = iota((168, 128), 0), iota((168, 128), 1)
+    within = row % 32
+    square = (row < 160) & (within % 8 < 6) & (source == 24 * (row // 32) + 6 * (within // 8) + within % 8)
+    plain = (row >= 160) & (source == row - 40)
+    mats = mm(jnp.where(square | plain, 1.0, 0.0), wide)
+    k, c = iota((32, 24), 0), iota((32, 24), 1)
+    pick = jnp.where((k % 8 < 6) & (c == 6 * (k // 8) + k % 8), 1.0, 0.0)
+    s_high, rest = split(stress)
+    s_mid, s_low = split(rest)
+    return mats, nt(pick, s_high) + nt(pick, s_mid) + nt(pick, s_low)
+
+
+def whole_kernel(
+    groups, rings, tiles, slot_far, span_far, factor_far, thick_far, weld_far, mode_far, adj_far,
+    membrane_far, bending_far, geometric_far, stress_far,
+    load_ref, grad_ref,
+    nodes_ref, index_ref, teff_ref, window_ref, near_ref, xy_ref, carry_out, carry_in,
+    plane_send, plane_recv, adj_send, adj_recv, rim_send, rim_recv, fwd_send, fwd_recv, carry_send, carry_recv,
+    slot_ref, span_ref, factor_ref, thick_ref, weld_ref, mode_ref, adj_ref,
+    membrane_ref, bending_ref, geometric_ref, stress_ref, input_sem,
 ):
-    member = lax.axis_index("mer")
-    factor = factor_ref[0]
+    mesh_id = pl.DeviceIdType.MESH
+    far = (mode_far, adj_far, slot_far, span_far, factor_far, thick_far, weld_far,
+           membrane_far, bending_far, geometric_far, stress_far)
+    close = (mode_ref, adj_ref, slot_ref, span_ref, factor_ref, thick_ref, weld_ref,
+             membrane_ref, bending_ref, geometric_ref, stress_ref)
+    inputs = [pltpu.make_async_copy(a, b, input_sem.at[n]) for n, (a, b) in enumerate(zip(far, close))]
+    for copy in inputs:
+        copy.start()
+    half_groups = groups // 2
+    ring, member = lax.axis_index("circ"), lax.axis_index("mer")
+    below, above = lax.rem(ring + rings - 1, rings), lax.rem(ring + 1, rings)
+    parity, pair_of = member % 2, member // 2
+    same = [2 * lax.rem(pair_of + i, half_groups) + parity for i in range(half_groups)]
+
+    barrier = pltpu.get_barrier_semaphore()
+    for d in range(1, groups):
+        pl.semaphore_signal(barrier, inc=1, device_id=(ring, lax.rem(member + d, groups)), device_id_type=mesh_id)
+    for i in range(half_groups):
+        pl.semaphore_signal(barrier, inc=1, device_id=(below, same[i]), device_id_type=mesh_id)
+        pl.semaphore_signal(barrier, inc=1, device_id=(above, same[i]), device_id_type=mesh_id)
+
+    for copy in inputs[:2]:
+        copy.wait()
+    empty = jnp.zeros((2, LANES), jnp.float32)
+    own = pl.multiple_of(member * WIDE, WIDE)
+    stride = 2 * tiles
+    for q in range(2):
+        for f in range(3):
+            for t in range(tiles):
+                six = mode_ref[pl.ds(f * 6 * stride + 2 * t + q, 6, stride=stride), :]
+                nodes_ref[q, 8 * f : 8 * f + 8, t * LANES : (t + 1) * LANES] = jnp.concatenate([six, empty], axis=0)
+        for t in range(2):
+            six = adj_ref[pl.ds(2 * t + q, 6, stride=4), :]
+            nodes_ref[q, 24:32, pl.ds(own + t * LANES, LANES)] = jnp.concatenate([six, empty], axis=0)
+    pl.semaphore_wait(barrier, groups - 1 + 2 * half_groups)
+
+    def block_of(owner):
+        return pl.ds(pl.multiple_of(owner * WIDE, WIDE), WIDE)
+
+    rims, adjs, planes, forwards = [], [], [], []
+    owners_same = [2 * lax.rem(pair_of + half_groups - i, half_groups) + parity for i in range(half_groups)]
+    for i in range(half_groups):
+        adjs.append(pltpu.make_async_remote_copy(
+            src_ref=nodes_ref.at[0, pl.ds(24, 8), block_of(member)],
+            dst_ref=nodes_ref.at[2, pl.ds(24, 8), block_of(member)],
+            send_sem=adj_send.at[i], recv_sem=adj_recv.at[i],
+            device_id=(below, same[i]), device_id_type=mesh_id))
+        rims.append(pltpu.make_async_remote_copy(
+            src_ref=nodes_ref.at[0, pl.ds(0, 24), block_of(owners_same[i])],
+            dst_ref=nodes_ref.at[2, pl.ds(0, 24), block_of(owners_same[i])],
+            send_sem=rim_send.at[i], recv_sem=rim_recv.at[i],
+            device_id=(below, member), device_id_type=mesh_id))
+        adjs[i].start()
+        rims[i].start()
+    for d in range(1, groups):
+        planes.append(pltpu.make_async_remote_copy(
+            src_ref=nodes_ref.at[pl.ds(0, 2), pl.ds(24, 8), block_of(member)],
+            dst_ref=nodes_ref.at[pl.ds(0, 2), pl.ds(24, 8), block_of(member)],
+            send_sem=plane_send.at[d], recv_sem=plane_recv.at[d],
+            device_id=(ring, lax.rem(member + d, groups)), device_id_type=mesh_id))
+        planes[-1].start()
+    for i in range(half_groups):
+        forwards.append(pltpu.make_async_remote_copy(
+            src_ref=nodes_ref.at[2, pl.ds(0, 32), block_of(owners_same[i])],
+            dst_ref=nodes_ref.at[2, pl.ds(0, 32), block_of(owners_same[i])],
+            send_sem=fwd_send.at[i], recv_sem=fwd_recv.at[i],
+            device_id=(ring, member + 1 - 2 * parity), device_id_type=mesh_id))
+
+    def send_on():
+        for i in range(half_groups):
+            adjs[i].wait_recv()
+            rims[i].wait_recv()
+            forwards[i].start()
+
+    for copy in inputs[2:]:
+        copy.wait()
+    factor = factor_ref[0, 0]
     start = jnp.int32(0)
     count = jnp.int32(0)
     for g in range(groups):
@@ -95,8 +200,7 @@
             for e, part in enumerate(untangle(natural_t, 0, lane + half * LANES, groups)):
                 teff_ref[cycle, 8 * e : 8 * e + 8, half * LANES : (half + 1) * LANES] = part
 
-    a_high, a_low = split(mats_ref[...])
-    mats = jnp.concatenate([a_high, a_low, a_high], axis=1)
+    mats, map_t = prepared_mats(membrane_ref[...], bending_ref[...], geometric_ref[...], stress_ref[...])
 
     owners, rows_of = [], []
     for d in (-1, 0, 1):
@@ -108,20 +212,21 @@
             row = jnp.where(member == groups - 1, pltpu.roll(row, WIDE - 1, 1), row)
         owners.append(owner)
         rows_of.append(row)
-    for d in range(3):
-        base = pl.multiple_of(owners[d] * WIDE, WIDE)
-        wide = jnp.broadcast_to(rows_of[d], (8, WIDE))
-        for half in range(2):
-            index = wide[:, half * LANES : (half + 1) * LANES]
-            low, in_low = index % LANES, index < LANES
-            for q in range(3):
-                for f in range(2):
-                    block = nodes_ref[q, 8 * f : 8 * f + 8, pl.ds(base, WIDE)]
-                    near_ref[q, 8 * f : 8 * f + 8, d * WIDE + half * LANES : d * WIDE + (half + 1) * LANES] = (
-                        gather_wide(block, low, in_low)
-                    )
-    loads = [jnp.zeros((8, WIDE), jnp.float32) for _ in range(3)]
-    for r in range(2):
+    def gather_near(cycles):
+        for d in range(3):
+            base = pl.multiple_of(owners[d] * WIDE, WIDE)
+            wide = jnp.broadcast_to(rows_of[d], (8, WIDE))
+            for half in range(2):
+                index = wide[:, half * LANES : (half + 1) * LANES]
+                low, in_low = index % LANES, index < LANES
+                for q in cycles:
+                    for f in range(2):
+                        block = nodes_ref[q, 8 * f : 8 * f + 8, pl.ds(base, WIDE)]
+                        near_ref[q, 8 * f : 8 * f + 8, d * WIDE + half * LANES : d * WIDE + (half + 1) * LANES] = (
+                            gather_wide(block, low, in_low)
+                        )
+
+    def cycle_loads(r):
         pair = [0.0, 0.0, 0.0]
         for f in range(2):
             rows = slice(8 * f, 8 * f + 8)
@@ -136,7 +241,7 @@
                 pair[s] = pair[s] + down(v * product[32 * s : 32 * s + 32])
         spread = 0.0
         for s in range(3):
-            spread = spread + map_ref[:, s : s + 1] * pair[s]
+            spread = spread + map_t[:, s : s + 1] * pair[s]
         behind = lax.rem(member + groups - 1, groups)
         te_here = teff_ref[r, pl.ds(member, 1), :]
         te_behind = teff_ref[r, pl.ds(behind, 1), :]
@@ -145,33 +250,23 @@
         from_here = spread[:, WIDE:] * (factor * te_here)
         loads[r] = loads[r] + from_here[0:8] + from_behind_[24:32]
         loads[r + 1] = loads[r + 1] + from_here[8:16] + from_behind_[16:24]
-    values = jnp.concatenate(loads, axis=0)
-    high, rest = split(values)
-    middle, low3 = split(rest)
-    place = (iota((WIDE, WIDE), 0) == jnp.broadcast_to(rows_of[1], (WIDE, WIDE))).astype(jnp.float32)
-    placed = lax.dot_general(
-        jnp.concatenate([high, middle, low3], axis=0), place, (((1,), (1,)), ((), ())),
-        preferred_element_type=jnp.float32,
-    )
-    placed = placed[0:24] + placed[24:48] + placed[48:72]
-    load_ref[0] = placed[0:8]
-    load_ref[1] = placed[8:16]
-    carry_ref[...] = placed[16:24]
-
-    for o in range(groups):
-        index = jnp.broadcast_to(shifted[o // 8][o % 8 : o % 8 + 1, :], (8, LANES))
-        low, in_low = index % LANES, index < LANES
-        for q in range(3):
-            for f in range(4):
-                block = nodes_ref[q, 8 * f : 8 * f + 8, o * WIDE : (o + 1) * WIDE]
-                got = gather_wide(block, low, in_low)
-                window_ref[q, 8 * f : 8 * f + 8, o * LANES : (o + 1) * LANES] = got
-                if o == 0:
-                    window_ref[q, 8 * f : 8 * f + 8, groups * LANES : (groups + 1) * LANES] = pltpu.roll(
-                        got, LANES - 1, 1
-                    )
+
+    def gather_window(cycles, fields):
+        for o in range(groups):
+            index = jnp.broadcast_to(shifted[o // 8][o % 8 : o % 8 + 1, :], (8, LANES))
+            low, in_low = index % LANES, index < LANES
+            for q in cycles:
+                for f in fields:
+                    block = nodes_ref[q, 8 * f : 8 * f + 8, o * WIDE : (o + 1) * WIDE]
+                    got = gather_wide(block, low, in_low)
+                    window_ref[q, 8 * f : 8 * f + 8, o * LANES : (o + 1) * LANES] = got
+                    if o == 0:
+                        window_ref[q, 8 * f : 8 * f + 8, groups * LANES : (groups + 1) * LANES] = pltpu.roll(
+                            got, LANES - 1, 1
+                        )
+
     size = 8 * LANES
-    for r in range(2):
+    def elements(r):
         for part in range(groups // 8):
             here = slice(part * size, (part + 1) * size)
             after = slice(part * size + LANES, (part + 1) * size + LANES)
@@ -204,6 +299,37 @@
                 cut = slice(o * LANES, (o + 1) * LANES)
                 xy_ref[2 * r, 8 * part + o : 8 * part + o + 1, :] = x[:, cut]
                 xy_ref[2 * r + 1, 8 * part + o : 8 * part + o + 1, :] = y[:, cut]
+
+    loads = [jnp.zeros((8, WIDE), jnp.float32) for _ in range(3)]
+    gather_near((0, 1))
+    cycle_loads(0)
+    send_on()
+    gather_window((0, 1), (0, 1, 2))
+    for copy in planes:
+        copy.wait_recv()
+    gather_window((0, 1), (3,))
+    elements(0)
+    for copy in forwards:
+        copy.wait_recv()
+    gather_near((2,))
+    cycle_loads(1)
+    values = jnp.concatenate(loads, axis=0)
+    high, rest = split(values)
+    middle, low3 = split(rest)
+    place = (iota((WIDE, WIDE), 0) == jnp.broadcast_to(rows_of[1], (WIDE, WIDE))).astype(jnp.float32)
+    placed = lax.dot_general(
+        jnp.concatenate([high, middle, low3], axis=0), place, (((1,), (1,)), ((), ())),
+        preferred_element_type=jnp.float32,
+    )
+    placed = placed[0:24] + placed[24:48] + placed[48:72]
+    carry_out[...] = placed[16:24]
+    carry = pltpu.make_async_remote_copy(
+        src_ref=carry_out, dst_ref=carry_in, send_sem=carry_send, recv_sem=carry_recv,
+        device_id=(above, member), device_id_type=mesh_id)
+    carry.start()
+
+    gather_window((2,), (0, 1, 2, 3))
+    elements(1)
 
     width = thick_ref.shape[1]
     back = lax.rem(width - start, width)
@@ -228,12 +354,12 @@
             g = growth_span[r : r + 1, cut] * (both[0] + 3.0 * te * te * both[1])
             grad_ref[r : r + 1, cut] = jnp.where(keep, g, 0.0)
 
-
-def padded_mats(membrane, bending, geometric, stress_map):
-    square = jnp.concatenate([membrane[None], bending[None], geometric], axis=0).reshape(5, 4, 6, 4, 6)
-    square = jnp.pad(square, ((0, 0), (0, 0), (0, 2), (0, 0), (0, 2))).reshape(160, 32)
-    rows = jnp.pad(stress_map.reshape(3, 4, 6), ((0, 5), (0, 0), (0, 2))).reshape(8, 32)
-    return jnp.concatenate([square, rows], axis=0), rows.T
+    carry.wait_recv()
+    load_ref[:, 0, :] = (placed[0:8] + carry_in[...])[0:6]
+    load_ref[:, 1, :] = placed[8:14]
+    carry.wait_send()
+    for copy in rims + adjs + planes + forwards:
+        copy.wait_send()
 
 
 def on_device(
@@ -244,39 +370,54 @@
     groups = lax.axis_size("mer")
     rings = lax.axis_size("circ")
     tiles = column_width // LANES
-    adj_column = lax.all_gather(adjoint, "mer", axis=2, tiled=True)
-    whole = jnp.concatenate([mode_fields, adj_column[None]], axis=0)
-    whole = jnp.pad(jnp.transpose(whole, (2, 0, 1, 3)), ((0, 0), (0, 0), (0, 2), (0, 0))).reshape(2, 32, column_width)
-    rim = lax.ppermute(whole[:1], "circ", [((i + 1) % rings, i) for i in range(rings)])
-    nodes = jnp.concatenate([whole, rim], axis=0)
-    mats, map_t = padded_mats(membrane, bending, geometric, stress_map)
+    mode_rows = mode_fields.reshape(3, 6, 2, tiles, LANES).transpose(0, 1, 3, 2, 4).reshape(-1, LANES)
+    adj_rows = adjoint.reshape(6, 2, 2, LANES).transpose(0, 2, 1, 3).reshape(-1, LANES)
     vmem = pl.BlockSpec(memory_space=pltpu.VMEM)
-    smem = pl.BlockSpec(memory_space=pltpu.SMEM)
-    load, carry, grad = pl.pallas_call(
-        functools.partial(local_kernel, groups, tiles),
+    hbm = pl.BlockSpec(memory_space=pltpu.HBM)
+    half_groups = groups // 2
+    dma = pltpu.SemaphoreType.DMA
+    return pl.pallas_call(
+        functools.partial(whole_kernel, groups, rings, tiles),
         out_shape=(
-            jax.ShapeDtypeStruct((2, 8, WIDE), jnp.float32),
-            jax.ShapeDtypeStruct((8, WIDE), jnp.float32),
+            jax.ShapeDtypeStruct((6, 2, WIDE), jnp.float32),
             jax.ShapeDtypeStruct((2, MOST), jnp.float32),
         ),
-        in_specs=[vmem, smem, smem, vmem, vmem, vmem, vmem, vmem],
-        out_specs=(vmem, vmem, vmem),
+        in_specs=[hbm] * 11,
+        out_specs=(vmem, vmem),
         scratch_shapes=[
+            pltpu.VMEM((3, 32, column_width), jnp.float32),
             pltpu.VMEM((groups, WIDE), jnp.int32),
             pltpu.VMEM((2, groups, WIDE), jnp.float32),
             pltpu.VMEM((3, 32, (groups + 1) * LANES), jnp.float32),
             pltpu.VMEM((3, 16, 3 * WIDE), jnp.float32),
             pltpu.VMEM((4, groups, LANES), jnp.float32),
+            pltpu.VMEM((8, WIDE), jnp.float32),
+            pltpu.VMEM((8, WIDE), jnp.float32),
+            dma((groups,)), dma((groups,)),
+            dma((half_groups,)), dma((half_groups,)),
+            dma((half_groups,)), dma((half_groups,)),
+            dma((half_groups,)), dma((half_groups,)),
+            dma, dma,
+            pltpu.VMEM((tiles, LANES), jnp.int32),
+            pltpu.SMEM((1, groups), jnp.int32),
+            pltpu.SMEM((1, 1), jnp.float32),
+            pltpu.VMEM((2, column_width), jnp.float32),
+            pltpu.VMEM((2, column_width), jnp.int32),
+            pltpu.VMEM(mode_rows.shape, jnp.float32),
+            pltpu.VMEM(adj_rows.shape, jnp.float32),
+            pltpu.VMEM((24, 24), jnp.float32),
+            pltpu.VMEM((24, 24), jnp.float32),
+            pltpu.VMEM((3, 24, 24), jnp.float32),
+            pltpu.VMEM((3, 24), jnp.float32),
+            dma((11,)),
         ],
-        compiler_params=pltpu.CompilerParams(vmem_limit_bytes=32 * 1024 * 1024),
+        compiler_params=pltpu.CompilerParams(
+            vmem_limit_bytes=60 * 1024 * 1024, collective_id=0, has_side_effects=True
+        ),
     )(
-        node_slot.reshape(tiles, LANES), panel_spans, load_factor.reshape(1), thickness, weld_land,
-        nodes, mats, map_t,
+        node_slot.reshape(tiles, LANES), panel_spans, load_factor.reshape(1, 1), thickness, weld_land,
+        mode_rows, adj_rows, membrane, bending, geometric, stress_map,
     )
-    carried = lax.ppermute(carry, "circ", [(i, (i + 1) % rings) for i in range(rings)])
-    load = load.at[0].add(carried)
-    adjoint_load = jnp.transpose(load[:, :6], (1, 0, 2))
-    return (adjoint_load, grad)
 
 
 def solution(mesh):

time: 33.3 us -> 21.3 us (0.64)
  Pallas kernels: 3.06 us -> 17.9 us
  blocking collectives: 10.6 us -> 0 us
  waiting for transfers between devices: 7.52 us -> 0 us
  starting transfers between devices: 4.11 us -> 0 us
  local copies, waits for them, and re-layouts: 4.63 us -> 1.91 us
  other arithmetic: 1.43 us -> 0 us
    pallas_call x1, Pallas kernels: 3.06 us -> 17.9 us  [on_device(): pl.pallas_call(functools.partial(whole_kernel, groups, rings, tiles), out...]
    all_gather x1 -> x0, blocking collectives: 10.6 us -> none  [on_device(): adj_column = lax.all_gather(adjoint, 'mer', axis=2, tiled=True)]
    ppermute x2 -> x0, waiting for transfers between devices: 7.52 us -> none  [the longest x1 5.45 us: on_device(): lax.ppermute(carry, 'circ', [(i, (i + 1) % rings) for i in range(rings)])]
    ppermute x2 -> x0, starting transfers between devices: 4.11 us -> none  [the longest x1 3.65 us: on_device(): lax.ppermute(whole[:1], 'circ', [((i + 1) % rings, i) for i in range(ring...]
    concatenate x7 -> x0, local copies, waits for them, and re-layouts: 1.22 us -> none  [the longest x6 1.12 us: padded_mats(): jnp.concatenate([membrane[None], bending[None], geometric], axis=0)]
    transpose x1 -> x0, other arithmetic: 1.18 us -> none  [on_device(): jnp.transpose(whole, (2, 0, 1, 3))]
    unnamed x20 -> x4, local copies, waits for them, and re-layouts: 2.93 us -> 1.91 us
  transfers between devices with their start and end apart: 2 -> 0, of which waited for: 2 -> 0; matrix products, arithmetic and copies ran while one was open for 6% -> 0% of each run, Pallas kernels for 0% -> 0%
where the time goes in v2:
time: 21.3 us; the launch traced here: 21.1 us
  Pallas kernels  17.9 us (84%)
  local copies, waits for them, and re-layouts  1.91 us (9%)
  between operations  1.3 us (6%)
    pallas_call x1, Pallas kernels, on_device(): pl.pallas_call(functools.partial(whole_kernel, groups, rings, tiles), out...  17.9 us
    unnamed x4, local copies, waits for them, and re-layouts  1.91 us

profile of v2, /device:TPU:0, one launch (start us, length us, event | category | flops | bytes accessed | tf_op | source)
XLA Modules:
  0.0 21.1 jit_solution(15643244414707722085)
XLA Ops:
  1.3 17.9 %shard_map.122 = (f32[6,2,256]{2,1,0:T(2,128)}, f32[2,768]{1,0:T(2,128)}) custom-call(s32[16,128]{1,0:T(8,128)} %bitcast.15, s32[1,8]{1,0:T(1,128)} %span_far.1, f32[1,1]{1,0:T(1,128)} %bitcast.12.factor_far, f32[2,2048]{1,0:T(2,128)} %thick_far.1, s32[2,2048]{1,0:T(2,128)} %weld_far.1, f32[576,128]{1,0:T(8,128)} %bitcast.13, f32[24,128]{1,0:T(8,128)} %bitcast.14, ...), custom_call_target="tpu_custom_call" | custom-call | tf_op jit(solution)/shard_map/pallas_call | solution.py:379
  19.1 0.0 copy-start
  19.2 1.3 %copy.18 = f32[6,2,256]{2,1,0:T(2,128)} copy(f32[6,2,256]{2,1,0:T(2,128)} %get-tuple-element.4) | data formatting | bytes 24576
  20.5 0.0 copy-done
  20.5 0.6 %copy.19 = f32[2,768]{1,0:T(2,128)} copy(f32[2,768]{1,0:T(2,128)S(1)} %copy-done) | data formatting | bytes 12288
Async XLA Ops:
  19.1 1.3 %copy-start = (f32[2,768]{1,0:T(2,128)S(1)}, f32[2,768]{1,0:T(2,128)}, u32[]{:S(2)}) copy-start(f32[2,768]{1,0:T(2,128)} %get-tuple-element.5) | copy-start | bytes 18436

commit v3 on v2

--- a/solution.py
+++ b/solution.py
@@ -92,7 +92,7 @@
     groups, rings, tiles, slot_far, span_far, factor_far, thick_far, weld_far, mode_far, adj_far,
     membrane_far, bending_far, geometric_far, stress_far,
     load_ref, grad_ref,
-    nodes_ref, index_ref, teff_ref, window_ref, near_ref, xy_ref, carry_out, carry_in,
+    nodes_ref, index_ref, teff_ref, window_ref, near_ref, xy_ref, te_out, te_in,
     plane_send, plane_recv, adj_send, adj_recv, rim_send, rim_recv, fwd_send, fwd_recv, carry_send, carry_recv,
     slot_ref, span_ref, factor_ref, thick_ref, weld_ref, mode_ref, adj_ref,
     membrane_ref, bending_ref, geometric_ref, stress_ref, input_sem,
@@ -123,14 +123,19 @@
     empty = jnp.zeros((2, LANES), jnp.float32)
     own = pl.multiple_of(member * WIDE, WIDE)
     stride = 2 * tiles
+    for f in range(4):
+        nodes_ref[2, f, 6:8, :] = jnp.zeros((2, tiles * LANES), jnp.float32)
+    for o in range(groups):
+        for q in range(2):
+            nodes_ref[q, 3, 6:8, o * WIDE : (o + 1) * WIDE] = jnp.zeros((2, WIDE), jnp.float32)
     for q in range(2):
         for f in range(3):
             for t in range(tiles):
                 six = mode_ref[pl.ds(f * 6 * stride + 2 * t + q, 6, stride=stride), :]
-                nodes_ref[q, 8 * f : 8 * f + 8, t * LANES : (t + 1) * LANES] = jnp.concatenate([six, empty], axis=0)
+                nodes_ref[q, f, :, t * LANES : (t + 1) * LANES] = jnp.concatenate([six, empty], axis=0)
         for t in range(2):
             six = adj_ref[pl.ds(2 * t + q, 6, stride=4), :]
-            nodes_ref[q, 24:32, pl.ds(own + t * LANES, LANES)] = jnp.concatenate([six, empty], axis=0)
+            nodes_ref[q, 3, 0:6, pl.ds(own + t * LANES, LANES)] = six
     pl.semaphore_wait(barrier, groups - 1 + 2 * half_groups)
 
     def block_of(owner):
@@ -140,28 +145,28 @@
     owners_same = [2 * lax.rem(pair_of + half_groups - i, half_groups) + parity for i in range(half_groups)]
     for i in range(half_groups):
         adjs.append(pltpu.make_async_remote_copy(
-            src_ref=nodes_ref.at[0, pl.ds(24, 8), block_of(member)],
-            dst_ref=nodes_ref.at[2, pl.ds(24, 8), block_of(member)],
+            src_ref=nodes_ref.at[0, pl.ds(3, 1), pl.ds(0, 6), block_of(member)],
+            dst_ref=nodes_ref.at[2, pl.ds(3, 1), pl.ds(0, 6), block_of(member)],
             send_sem=adj_send.at[i], recv_sem=adj_recv.at[i],
             device_id=(below, same[i]), device_id_type=mesh_id))
         rims.append(pltpu.make_async_remote_copy(
-            src_ref=nodes_ref.at[0, pl.ds(0, 24), block_of(owners_same[i])],
-            dst_ref=nodes_ref.at[2, pl.ds(0, 24), block_of(owners_same[i])],
+            src_ref=nodes_ref.at[0, pl.ds(0, 3), pl.ds(0, 6), block_of(owners_same[i])],
+            dst_ref=nodes_ref.at[2, pl.ds(0, 3), pl.ds(0, 6), block_of(owners_same[i])],
             send_sem=rim_send.at[i], recv_sem=rim_recv.at[i],
             device_id=(below, member), device_id_type=mesh_id))
         adjs[i].start()
         rims[i].start()
     for d in range(1, groups):
         planes.append(pltpu.make_async_remote_copy(
-            src_ref=nodes_ref.at[pl.ds(0, 2), pl.ds(24, 8), block_of(member)],
-            dst_ref=nodes_ref.at[pl.ds(0, 2), pl.ds(24, 8), block_of(member)],
+            src_ref=nodes_ref.at[pl.ds(0, 2), pl.ds(3, 1), pl.ds(0, 6), block_of(member)],
+            dst_ref=nodes_ref.at[pl.ds(0, 2), pl.ds(3, 1), pl.ds(0, 6), block_of(member)],
             send_sem=plane_send.at[d], recv_sem=plane_recv.at[d],
             device_id=(ring, lax.rem(member + d, groups)), device_id_type=mesh_id))
         planes[-1].start()
     for i in range(half_groups):
         forwards.append(pltpu.make_async_remote_copy(
-            src_ref=nodes_ref.at[2, pl.ds(0, 32), block_of(owners_same[i])],
-            dst_ref=nodes_ref.at[2, pl.ds(0, 32), block_of(owners_same[i])],
+            src_ref=nodes_ref.at[2, pl.ds(0, 4), pl.ds(0, 6), block_of(owners_same[i])],
+            dst_ref=nodes_ref.at[2, pl.ds(0, 4), pl.ds(0, 6), block_of(owners_same[i])],
             send_sem=fwd_send.at[i], recv_sem=fwd_recv.at[i],
             device_id=(ring, member + 1 - 2 * parity), device_id_type=mesh_id))
 
@@ -221,20 +226,27 @@
                 low, in_low = index % LANES, index < LANES
                 for q in cycles:
                     for f in range(2):
-                        block = nodes_ref[q, 8 * f : 8 * f + 8, pl.ds(base, WIDE)]
+                        block = nodes_ref[q, f, :, pl.ds(base, WIDE)]
                         near_ref[q, 8 * f : 8 * f + 8, d * WIDE + half * LANES : d * WIDE + (half + 1) * LANES] = (
                             gather_wide(block, low, in_low)
                         )
 
-    def cycle_loads(r):
+    behind = lax.rem(member + groups - 1, groups)
+
+    def te_of(r):
+        te_behind = teff_ref[r, pl.ds(behind, 1), :]
+        te_behind = jnp.where(member == 0, pltpu.roll(te_behind, 1, 1), te_behind)
+        return jnp.concatenate([te_behind, teff_ref[r, pl.ds(member, 1), :]], axis=1)
+
+    def cycle_loads(lower, upper, te):
         pair = [0.0, 0.0, 0.0]
         for f in range(2):
             rows = slice(8 * f, 8 * f + 8)
             v = stack_corners(
-                near_ref[r, rows, : 2 * WIDE],
-                near_ref[r + 1, rows, : 2 * WIDE],
-                near_ref[r + 1, rows, WIDE:],
-                near_ref[r, rows, WIDE:],
+                near_ref[lower, rows, : 2 * WIDE],
+                near_ref[upper, rows, : 2 * WIDE],
+                near_ref[upper, rows, WIDE:],
+                near_ref[lower, rows, WIDE:],
             )
             product = mm(mats[64:160], triple(v))
             for s in range(3):
@@ -242,14 +254,11 @@
         spread = 0.0
         for s in range(3):
             spread = spread + map_t[:, s : s + 1] * pair[s]
-        behind = lax.rem(member + groups - 1, groups)
-        te_here = teff_ref[r, pl.ds(member, 1), :]
-        te_behind = teff_ref[r, pl.ds(behind, 1), :]
-        te_behind = jnp.where(member == 0, pltpu.roll(te_behind, 1, 1), te_behind)
-        from_behind_ = spread[:, :WIDE] * (factor * te_behind)
-        from_here = spread[:, WIDE:] * (factor * te_here)
-        loads[r] = loads[r] + from_here[0:8] + from_behind_[24:32]
-        loads[r + 1] = loads[r + 1] + from_here[8:16] + from_behind_[16:24]
+        spread = spread * (factor * te)
+        return (
+            spread[0:8, WIDE:] + spread[24:32, :WIDE],
+            spread[8:16, WIDE:] + spread[16:24, :WIDE],
+        )
 
     def gather_window(cycles, fields):
         for o in range(groups):
@@ -257,7 +266,7 @@
             low, in_low = index % LANES, index < LANES
             for q in cycles:
                 for f in fields:
-                    block = nodes_ref[q, 8 * f : 8 * f + 8, o * WIDE : (o + 1) * WIDE]
+                    block = nodes_ref[q, f, :, o * WIDE : (o + 1) * WIDE]
                     got = gather_wide(block, low, in_low)
                     window_ref[q, 8 * f : 8 * f + 8, o * LANES : (o + 1) * LANES] = got
                     if o == 0:
@@ -300,34 +309,43 @@
                 xy_ref[2 * r, 8 * part + o : 8 * part + o + 1, :] = x[:, cut]
                 xy_ref[2 * r + 1, 8 * part + o : 8 * part + o + 1, :] = y[:, cut]
 
-    loads = [jnp.zeros((8, WIDE), jnp.float32) for _ in range(3)]
-    gather_near((0, 1))
-    cycle_loads(0)
+    gather_near((1,))
+    te_rows = te_of(1)
+    te_out[...] = jnp.concatenate(
+        [te_rows[:, n * LANES : (n + 1) * LANES] for n in range(4)] + [jnp.zeros((4, LANES), jnp.float32)], axis=0
+    )
+    upward = [
+        pltpu.make_async_remote_copy(
+            src_ref=src, dst_ref=dst, send_sem=carry_send.at[n], recv_sem=carry_recv.at[n],
+            device_id=(above, member), device_id_type=mesh_id)
+        for n, (src, dst) in enumerate(((near_ref.at[1], near_ref.at[3]), (te_out, te_in)))
+    ]
+    for copy in upward:
+        copy.start()
+    gather_near((0,))
+    lower0, upper0 = cycle_loads(0, 1, te_of(0))
     send_on()
     gather_window((0, 1), (0, 1, 2))
     for copy in planes:
         copy.wait_recv()
     gather_window((0, 1), (3,))
     elements(0)
+    for copy in upward:
+        copy.wait_recv()
+    te_below = jnp.concatenate([te_in[n : n + 1, :] for n in range(4)], axis=1)
+    _, upper_below = cycle_loads(3, 0, te_below)
     for copy in forwards:
         copy.wait_recv()
     gather_near((2,))
-    cycle_loads(1)
-    values = jnp.concatenate(loads, axis=0)
+    lower1, _ = cycle_loads(1, 2, te_rows)
+    values = jnp.concatenate([lower0 + upper_below, lower1 + upper0], axis=0)
     high, rest = split(values)
     middle, low3 = split(rest)
     place = (iota((WIDE, WIDE), 0) == jnp.broadcast_to(rows_of[1], (WIDE, WIDE))).astype(jnp.float32)
-    placed = lax.dot_general(
-        jnp.concatenate([high, middle, low3], axis=0), place, (((1,), (1,)), ((), ())),
-        preferred_element_type=jnp.float32,
-    )
-    placed = placed[0:24] + placed[24:48] + placed[48:72]
-    carry_out[...] = placed[16:24]
-    carry = pltpu.make_async_remote_copy(
-        src_ref=carry_out, dst_ref=carry_in, send_sem=carry_send, recv_sem=carry_recv,
-        device_id=(above, member), device_id_type=mesh_id)
-    carry.start()
-
+    placed = nt(jnp.concatenate([high, middle, low3], axis=0), place)
+    placed = placed[0:16] + placed[16:32] + placed[32:48]
+    load_ref[:, 0, :] = placed[0:6]
+    load_ref[:, 1, :] = placed[8:14]
     gather_window((2,), (0, 1, 2, 3))
     elements(1)
 
@@ -354,11 +372,7 @@
             g = growth_span[r : r + 1, cut] * (both[0] + 3.0 * te * te * both[1])
             grad_ref[r : r + 1, cut] = jnp.where(keep, g, 0.0)
 
-    carry.wait_recv()
-    load_ref[:, 0, :] = (placed[0:8] + carry_in[...])[0:6]
-    load_ref[:, 1, :] = placed[8:14]
-    carry.wait_send()
-    for copy in rims + adjs + planes + forwards:
+    for copy in rims + adjs + planes + forwards + upward:
         copy.wait_send()
 
 
@@ -385,19 +399,19 @@
         in_specs=[hbm] * 11,
         out_specs=(vmem, vmem),
         scratch_shapes=[
-            pltpu.VMEM((3, 32, column_width), jnp.float32),
+            pltpu.VMEM((3, 4, 8, column_width), jnp.float32),
             pltpu.VMEM((groups, WIDE), jnp.int32),
             pltpu.VMEM((2, groups, WIDE), jnp.float32),
             pltpu.VMEM((3, 32, (groups + 1) * LANES), jnp.float32),
-            pltpu.VMEM((3, 16, 3 * WIDE), jnp.float32),
+            pltpu.VMEM((4, 16, 3 * WIDE), jnp.float32),
             pltpu.VMEM((4, groups, LANES), jnp.float32),
-            pltpu.VMEM((8, WIDE), jnp.float32),
-            pltpu.VMEM((8, WIDE), jnp.float32),
+            pltpu.VMEM((8, LANES), jnp.float32),
+            pltpu.VMEM((8, LANES), jnp.float32),
             dma((groups,)), dma((groups,)),
             dma((half_groups,)), dma((half_groups,)),
             dma((half_groups,)), dma((half_groups,)),
             dma((half_groups,)), dma((half_groups,)),
-            dma, dma,
+            dma((2,)), dma((2,)),
             pltpu.VMEM((tiles, LANES), jnp.int32),
             pltpu.SMEM((1, groups), jnp.int32),
             pltpu.SMEM((1, 1), jnp.float32),

time: 21.3 us -> 17.3 us (0.81)
  Pallas kernels: 17.9 us -> 13.9 us
    pallas_call x1, Pallas kernels: 17.9 us -> 13.9 us  [on_device(): pl.pallas_call(functools.partial(whole_kernel, groups, rings, tiles), out...]
where the time goes in v3:
time: 17.3 us; the launch traced here: 17.1 us
  Pallas kernels  13.9 us (80%)
  local copies, waits for them, and re-layouts  1.91 us (11%)
  between operations  1.3 us (8%)
    pallas_call x1, Pallas kernels, on_device(): pl.pallas_call(functools.partial(whole_kernel, groups, rings, tiles), out...  13.9 us
    unnamed x4, local copies, waits for them, and re-layouts  1.91 us

profile of v3, /device:TPU:0, one launch (start us, length us, event | category | flops | bytes accessed | tf_op | source)
XLA Modules:
  0.0 17.1 jit_solution(6194731057672941420)
XLA Ops:
  1.3 13.9 %shard_map.122 = (f32[6,2,256]{2,1,0:T(2,128)}, f32[2,768]{1,0:T(2,128)}) custom-call(s32[16,128]{1,0:T(8,128)} %bitcast.15, s32[1,8]{1,0:T(1,128)} %span_far.1, f32[1,1]{1,0:T(1,128)} %bitcast.12.factor_far, f32[2,2048]{1,0:T(2,128)} %thick_far.1, s32[2,2048]{1,0:T(2,128)} %weld_far.1, f32[576,128]{1,0:T(8,128)} %bitcast.13, f32[24,128]{1,0:T(8,128)} %bitcast.14, ...), custom_call_target="tpu_custom_call" | custom-call | tf_op jit(solution)/shard_map/pallas_call | solution.py:393
  15.2 0.0 copy-start
  15.2 1.3 %copy.18 = f32[6,2,256]{2,1,0:T(2,128)} copy(f32[6,2,256]{2,1,0:T(2,128)} %get-tuple-element.4) | data formatting | bytes 24576
  16.5 0.0 copy-done
  16.5 0.6 %copy.19 = f32[2,768]{1,0:T(2,128)} copy(f32[2,768]{1,0:T(2,128)S(1)} %copy-done) | data formatting | bytes 12288
Async XLA Ops:
  15.2 1.3 %copy-start = (f32[2,768]{1,0:T(2,128)S(1)}, f32[2,768]{1,0:T(2,128)}, u32[]{:S(2)}) copy-start(f32[2,768]{1,0:T(2,128)} %get-tuple-element.5) | copy-start | bytes 18436

commit v4 on v3

--- a/solution.py
+++ b/solution.py
@@ -91,7 +91,7 @@
 def whole_kernel(
     groups, rings, tiles, slot_far, span_far, factor_far, thick_far, weld_far, mode_far, adj_far,
     membrane_far, bending_far, geometric_far, stress_far,
-    load_ref, grad_ref,
+    packed_ref,
     nodes_ref, index_ref, teff_ref, window_ref, near_ref, xy_ref, te_out, te_in,
     plane_send, plane_recv, adj_send, adj_recv, rim_send, rim_recv, fwd_send, fwd_recv, carry_send, carry_recv,
     slot_ref, span_ref, factor_ref, thick_ref, weld_ref, mode_ref, adj_ref,
@@ -123,6 +123,8 @@
     empty = jnp.zeros((2, LANES), jnp.float32)
     own = pl.multiple_of(member * WIDE, WIDE)
     stride = 2 * tiles
+    for f in range(2):
+        near_ref[3, f, 6:8, :] = jnp.zeros((2, 3 * WIDE), jnp.float32)
     for f in range(4):
         nodes_ref[2, f, 6:8, :] = jnp.zeros((2, tiles * LANES), jnp.float32)
     for o in range(groups):
@@ -227,7 +229,7 @@
                 for q in cycles:
                     for f in range(2):
                         block = nodes_ref[q, f, :, pl.ds(base, WIDE)]
-                        near_ref[q, 8 * f : 8 * f + 8, d * WIDE + half * LANES : d * WIDE + (half + 1) * LANES] = (
+                        near_ref[q, f, :, d * WIDE + half * LANES : d * WIDE + (half + 1) * LANES] = (
                             gather_wide(block, low, in_low)
                         )
 
@@ -241,12 +243,11 @@
     def cycle_loads(lower, upper, te):
         pair = [0.0, 0.0, 0.0]
         for f in range(2):
-            rows = slice(8 * f, 8 * f + 8)
             v = stack_corners(
-                near_ref[lower, rows, : 2 * WIDE],
-                near_ref[upper, rows, : 2 * WIDE],
-                near_ref[upper, rows, WIDE:],
-                near_ref[lower, rows, WIDE:],
+                near_ref[lower, f, :, : 2 * WIDE],
+                near_ref[upper, f, :, : 2 * WIDE],
+                near_ref[upper, f, :, WIDE:],
+                near_ref[lower, f, :, WIDE:],
             )
             product = mm(mats[64:160], triple(v))
             for s in range(3):
@@ -318,7 +319,9 @@
         pltpu.make_async_remote_copy(
             src_ref=src, dst_ref=dst, send_sem=carry_send.at[n], recv_sem=carry_recv.at[n],
             device_id=(above, member), device_id_type=mesh_id)
-        for n, (src, dst) in enumerate(((near_ref.at[1], near_ref.at[3]), (te_out, te_in)))
+        for n, (src, dst) in enumerate((
+            (near_ref.at[1, pl.ds(0, 2), pl.ds(0, 6)], near_ref.at[3, pl.ds(0, 2), pl.ds(0, 6)]), (te_out, te_in),
+        ))
     ]
     for copy in upward:
         copy.start()
@@ -344,8 +347,10 @@
     place = (iota((WIDE, WIDE), 0) == jnp.broadcast_to(rows_of[1], (WIDE, WIDE))).astype(jnp.float32)
     placed = nt(jnp.concatenate([high, middle, low3], axis=0), place)
     placed = placed[0:16] + placed[16:32] + placed[32:48]
-    load_ref[:, 0, :] = placed[0:6]
-    load_ref[:, 1, :] = placed[8:14]
+    for q in range(2):
+        for h in range(2):
+            at = 16 * q + 8 * h
+            packed_ref[at : at + 8, :] = placed[8 * q : 8 * q + 8, h * LANES : (h + 1) * LANES]
     gather_window((2,), (0, 1, 2, 3))
     elements(1)
 
@@ -370,10 +375,23 @@
                 both.append(total)
             te = te_span[r : r + 1, cut]
             g = growth_span[r : r + 1, cut] * (both[0] + 3.0 * te * te * both[1])
-            grad_ref[r : r + 1, cut] = jnp.where(keep, g, 0.0)
+            at = 32 + r * (MOST // LANES) + b
+            packed_ref[at : at + 1, :] = jnp.where(keep, g, 0.0)
 
     for copy in rims + adjs + planes + forwards + upward:
         copy.wait_send()
+
+
+def unpack_kernel(packed_ref, load_ref, grad_ref):
+    blocks = MOST // LANES
+    for q in range(2):
+        for h in range(2):
+            at = 16 * q + 8 * h
+            load_ref[:, q, h * LANES : (h + 1) * LANES] = packed_ref[at : at + 6, :]
+    for r in range(2):
+        for b in range(blocks):
+            at = 32 + r * blocks + b
+            grad_ref[r : r + 1, b * LANES : (b + 1) * LANES] = packed_ref[at : at + 1, :]
 
 
 def on_device(
@@ -390,20 +408,17 @@
     hbm = pl.BlockSpec(memory_space=pltpu.HBM)
     half_groups = groups // 2
     dma = pltpu.SemaphoreType.DMA
-    return pl.pallas_call(
+    packed = pl.pallas_call(
         functools.partial(whole_kernel, groups, rings, tiles),
-        out_shape=(
-            jax.ShapeDtypeStruct((6, 2, WIDE), jnp.float32),
-            jax.ShapeDtypeStruct((2, MOST), jnp.float32),
-        ),
+        out_shape=jax.ShapeDtypeStruct((32 + 2 * MOST // LANES, LANES), jnp.float32),
         in_specs=[hbm] * 11,
-        out_specs=(vmem, vmem),
+        out_specs=vmem,
         scratch_shapes=[
             pltpu.VMEM((3, 4, 8, column_width), jnp.float32),
             pltpu.VMEM((groups, WIDE), jnp.int32),
             pltpu.VMEM((2, groups, WIDE), jnp.float32),
             pltpu.VMEM((3, 32, (groups + 1) * LANES), jnp.float32),
-            pltpu.VMEM((4, 16, 3 * WIDE), jnp.float32),
+            pltpu.VMEM((4, 2, 8, 3 * WIDE), jnp.float32),
             pltpu.VMEM((4, groups, LANES), jnp.float32),
             pltpu.VMEM((8, LANES), jnp.float32),
             pltpu.VMEM((8, LANES), jnp.float32),
@@ -432,6 +447,15 @@
         node_slot.reshape(tiles, LANES), panel_spans, load_factor.reshape(1, 1), thickness, weld_land,
         mode_rows, adj_rows, membrane, bending, geometric, stress_map,
     )
+    return pl.pallas_call(
+        unpack_kernel,
+        out_shape=(
+            jax.ShapeDtypeStruct((6, 2, WIDE), jnp.float32),
+            jax.ShapeDtypeStruct((2, MOST), jnp.float32),
+        ),
+        in_specs=[vmem],
+        out_specs=(vmem, vmem),
+    )(packed)
 
 
 def solution(mesh):

time: 17.3 us -> 16.5 us (0.954)
  local copies, waits for them, and re-layouts: 1.91 us -> 0 us
  Pallas kernels: 13.9 us -> 15 us
    unnamed x4 -> x0, local copies, waits for them, and re-layouts: 1.91 us -> none
    pallas_call x0 -> x1, Pallas kernels: none -> 1.35 us  [on_device(): pl.pallas_call(unpack_kernel, out_shape=(jax.ShapeDtypeStruct((6, 2, WIDE...]
    pallas_call x1, Pallas kernels: 13.9 us -> 13.6 us  [on_device(): pl.pallas_call(functools.partial(whole_kernel, groups, rings, tiles), out...]
where the time goes in v4:
time: 16.5 us; the launch traced here: 16.2 us
  Pallas kernels  15 us (91%)
  between operations  1.29 us (8%)
    pallas_call x1, Pallas kernels, on_device(): pl.pallas_call(functools.partial(whole_kernel, groups, rings, tiles), out...  13.6 us
    pallas_call x1, Pallas kernels, on_device(): pl.pallas_call(unpack_kernel, out_shape=(jax.ShapeDtypeStruct((6, 2, WIDE...  1.35 us

profile of v4, /device:TPU:0, one launch (start us, length us, event | category | flops | bytes accessed | tf_op | source)
XLA Modules:
  0.0 16.2 jit_solution(5191212016802811526)
XLA Ops:
  1.3 13.6 %shard_map.122.packed_ref = f32[44,128]{1,0:T(8,128)} custom-call(s32[16,128]{1,0:T(8,128)} %bitcast.15, s32[1,8]{1,0:T(1,128)} %span_far.1, f32[1,1]{1,0:T(1,128)} %bitcast.12.factor_far, f32[2,2048]{1,0:T(2,128)} %thick_far.1, s32[2,2048]{1,0:T(2,128)} %weld_far.1, f32[576,128]{1,0:T(8,128)} %bitcast.13, f32[24,128]{1,0:T(8,128)} %bitcast.14, ...), custom_call_target="tpu_custom_call" | custom-call | tf_op jit(solution)/shard_map/pallas_call | solution.py:411
  14.9 1.4 %shard_map.123 = (f32[6,2,256]{2,1,0:T(2,128)}, f32[2,768]{1,0:T(2,128)}) custom-call(f32[44,128]{1,0:T(8,128)} %shard_map.122.packed_ref), custom_call_target="tpu_custom_call" | custom-call | tf_op jit(solution)/shard_map/pallas_call | solution.py:450

commit v5 on v4

--- a/solution.py
+++ b/solution.py
@@ -156,8 +156,8 @@
             dst_ref=nodes_ref.at[2, pl.ds(0, 3), pl.ds(0, 6), block_of(owners_same[i])],
             send_sem=rim_send.at[i], recv_sem=rim_recv.at[i],
             device_id=(below, member), device_id_type=mesh_id))
+        rims[i].start()
         adjs[i].start()
-        rims[i].start()
     for d in range(1, groups):
         planes.append(pltpu.make_async_remote_copy(
             src_ref=nodes_ref.at[pl.ds(0, 2), pl.ds(3, 1), pl.ds(0, 6), block_of(member)],
@@ -327,8 +327,8 @@
         copy.start()
     gather_near((0,))
     lower0, upper0 = cycle_loads(0, 1, te_of(0))
+    gather_window((0, 1), (0, 1, 2))
     send_on()
-    gather_window((0, 1), (0, 1, 2))
     for copy in planes:
         copy.wait_recv()
     gather_window((0, 1), (3,))

time: 16.5 us -> 16.5 us (level)
  no operation moved by 1% of the time
where the time goes in v5:
time: 16.5 us; the launch traced here: 16.2 us
  Pallas kernels  15 us (91%)
  between operations  1.29 us (8%)
    pallas_call x1, Pallas kernels, on_device(): pl.pallas_call(functools.partial(whole_kernel, groups, rings, tiles), out...  13.6 us
    pallas_call x1, Pallas kernels, on_device(): pl.pallas_call(unpack_kernel, out_shape=(jax.ShapeDtypeStruct((6, 2, WIDE...  1.35 us

profile of v5, /device:TPU:0, one launch (start us, length us, event | category | flops | bytes accessed | tf_op | source)
XLA Modules:
  0.0 16.2 jit_solution(7687611646632651728)
XLA Ops:
  1.3 13.6 %shard_map.122.packed_ref = f32[44,128]{1,0:T(8,128)} custom-call(s32[16,128]{1,0:T(8,128)} %bitcast.15, s32[1,8]{1,0:T(1,128)} %span_far.1, f32[1,1]{1,0:T(1,128)} %bitcast.12.factor_far, f32[2,2048]{1,0:T(2,128)} %thick_far.1, s32[2,2048]{1,0:T(2,128)} %weld_far.1, f32[576,128]{1,0:T(8,128)} %bitcast.13, f32[24,128]{1,0:T(8,128)} %bitcast.14, ...), custom_call_target="tpu_custom_call" | custom-call | tf_op jit(solution)/shard_map/pallas_call | solution.py:411
  14.9 1.4 %shard_map.123 = (f32[6,2,256]{2,1,0:T(2,128)}, f32[2,768]{1,0:T(2,128)}) custom-call(f32[44,128]{1,0:T(8,128)} %shard_map.122.packed_ref), custom_call_target="tpu_custom_call" | custom-call | tf_op jit(solution)/shard_map/pallas_call | solution.py:450
